TPU v7x, 32 devices: a whole 2x2x4 slice. The times are simulated.
32 devices in a mesh: band: 2 (over y), domain: 16 (over z, x, core).
Axes of the slice: x: 2, y: 2, z: 4, core: 2. Of those that a mesh axis runs over, the one named last changes fastest.
Arguments:
- targets: float32 [4, 36864, 192], P('band', 'domain'), may hold values from -5 to 5
- partner_pool: bfloat16 [64, 36864, 192], P('band', 'domain'), may hold values from -5 to 5
- owners: int32 [2], replicated, may hold values from 0 to 1, as said below
- warm_start: bfloat16 [2, 8, 4, 36864, 192], P(None, None, 'band', 'domain'), may hold values from -6 to 6
Outputs:
- exchange: float32 [4, 36864, 192], P('band', 'domain')
Inputs may be any that keep to these rules, and one draw needn't show every extreme that they name: The 2 broadcast blocks have distinct owners.
All inputs are finite; a program needn't handle non-finite values.
Results may differ from a plain program's by a relative error of at most 0.0006.
Values may be sent and summed in bfloat16 or wider, within the bound.
A program may use at most 576 MiB of HBM per device.

v0:
```python
import math

import jax
import jax.numpy as jnp
from jax import lax
from jax.sharding import PartitionSpec as P

ORB = 8
STEPS = 2
SWEEPS = 3
GX = 192
GY = 192
GZ = 192


coupling = 4.0 * math.pi


def spread(block, axis, owner):
    block = jnp.where(lax.axis_index(axis) == owner, block, jnp.zeros_like(block))
    return lax.psum(block, axis)


def padded(block, sides, width):
    for axis, dim in sides:
        count = lax.axis_size(axis)
        forward = [(i, i + 1) for i in range(count - 1)]
        forward.append((count - 1, 0))
        backward = [(target, source) for source, target in forward]
        low = lax.ppermute(
            lax.slice_in_dim(block, block.shape[dim] - width, None, axis=dim), axis, forward
        )
        high = lax.ppermute(lax.slice_in_dim(block, 0, width, axis=dim), axis, backward)
        block = jnp.concatenate([low, block, high], axis=dim)
    return block


def row_sweep(widened, source, first_row):
    row_count = source.shape[1]
    line = GY
    centre = widened[:, line : line + row_count]
    beside = widened[:, :row_count] + widened[:, 2 * line : 2 * line + row_count]
    column = (first_row + jnp.arange(row_count, dtype=jnp.int32)) % line
    at_end = (column == line - 1)[None, :, None]
    at_start = (column == 0)[None, :, None]
    upper = jnp.where(
        at_end, widened[:, 1 : row_count + 1], widened[:, line + 1 : line + row_count + 1]
    )
    lower = jnp.where(
        at_start,
        widened[:, 2 * line - 1 : 2 * line - 1 + row_count],
        widened[:, line - 1 : line - 1 + row_count],
    )
    beside = beside + upper + lower + jnp.roll(centre, 1, 2) + jnp.roll(centre, -1, 2)
    return (beside + coupling * source) / 6.0


def fetch_block(partner_pool, owners, block_index):
    own_block = partner_pool[block_index * ORB : (block_index + 1) * ORB]
    return spread(own_block, "band", owners[block_index]).astype(jnp.float32)


def pair_products(partner, targets):
    density = partner[:, None] * targets[None]
    return (density, jnp.sum(density, axis=(2, 3)))


def solve_block(partner, density, mean_value, warm_block, first_row):
    block_width = partner.shape[0]
    target_count = density.shape[1]
    pair_count = block_width * target_count
    planes = density.shape[2:]
    source = density.reshape((pair_count,) + planes) - mean_value.reshape(pair_count, 1, 1)
    potential = warm_block.reshape((pair_count,) + planes).astype(jnp.float32)
    for sweep_index in range(SWEEPS):
        widened = padded(potential.astype(jnp.bfloat16), (("domain", 1),), GY).astype(
            potential.dtype
        )
        potential = row_sweep(widened, source, first_row)
    potential = potential.reshape((block_width, target_count) + planes)
    return jnp.sum(potential * partner[:, None], axis=0)


def body(targets, partner_pool, owners, warm_start):
    row_count = targets.shape[1]
    first_row = lax.axis_index("domain") * row_count
    cell_count = GX * GY * GZ
    exchange = jnp.zeros(targets.shape, jnp.float32)
    for block_index in range(STEPS):
        partner = fetch_block(partner_pool, owners, block_index)
        density, local_sums = pair_products(partner, targets)
        totals = lax.psum(local_sums, "domain")
        exchange = exchange - solve_block(
            partner, density, totals / cell_count, warm_start[block_index], first_row
        )
    return exchange


def solution(mesh):
    return jax.shard_map(
        body,
        mesh=mesh,
        in_specs=(
            P("band", "domain", None),
            P("band", "domain", None),
            P(),
            P(None, None, "band", "domain", None),
        ),
        out_specs=P("band", "domain", None),
        check_vma=False,
    )
```

profile of v0, /device:TPU:1, one launch (start us, length us, event | category | flops | bytes accessed | tf_op | source)
XLA Modules:
  0.0 1326.7 jit_solution(8295854403354651101)
XLA Ops:
  44.8 42.7 %collective-permute-done = bf16[16,192,192]{1,2,0:T(8,128)(2,1)S(1)} collective-permute-done((bf16[16,192,192]{1,2,0:T(8,128)(2,1)}, bf16[16,192,192]{1,2,0:T(8,128)(2,1)S(1)}, u32[]{:S(2)}, u32[]{:S(2)}) %collective-permute-start) | collective-permute-done | bytes 1179680 | tf_op jit(solution)/shard_map/ppermute | solution.py:30
  90.3 29.5 %concatenate.56 = bf16[16,2688,192]{1,2,0:T(8,128)(2,1)} concatenate(bf16[16,192,192]{1,2,0:T(8,128)(2,1)S(1)} %collective-permute-done, bf16[16,2304,192]{1,2,0:T(8,128)(2,1)} %bitcast.31, bf16[16,192,192]{1,2,0:T(8,128)(2,1)} %collective-permute-done.1), dimensions={1} | concatenate | bytes 33030144 | tf_op jit(solution)/shard_map/concatenate | solution.py:34
  119.8 18.4 %convert_element_type.40 = f32[16,2688,192]{1,2,0:T(8,128)} convert(bf16[16,2688,192]{1,2,0:T(8,128)(2,1)} %concatenate.56) | non-fusion elementwise | flops 8257536 | bytes 49545216 | tf_op jit(solution)/shard_map/convert_element_type | solution.py:76
  138.2 29.4 %concatenate.65 = bf16[16,2688,192]{1,2,0:T(8,128)(2,1)} concatenate(bf16[16,192,192]{1,2,0:T(8,128)(2,1)S(1)} %collective-permute-done.6, bf16[16,2304,192]{1,2,0:T(8,128)(2,1)} %bitcast.29, bf16[16,192,192]{1,2,0:T(8,128)(2,1)} %collective-permute-done.7), dimensions={1} | concatenate | bytes 33030144 | tf_op jit(solution)/shard_map/concatenate | solution.py:34
  167.6 18.9 %convert_element_type.46 = f32[16,2688,192]{1,2,0:T(8,128)} convert(bf16[16,2688,192]{1,2,0:T(8,128)(2,1)} %concatenate.65) | non-fusion elementwise | flops 8257536 | bytes 49545216 | tf_op jit(solution)/shard_map/convert_element_type | solution.py:76
  192.7 31.5 %fusion.54 = (f32[16,2304,191]{1,2,0:T(8,128)}, f32[16,2304,191]{1,2,0:T(8,128)}) fusion(bf16[16,2688,192]{1,2,0:T(8,128)(2,1)} %concatenate.56), kind=kLoop, calls=%fused_computation.85 | loop fusion | bytes 112656384 | tf_op jit(solution)/shard_map/jit(_roll_static)/slice | solution.py:54
  224.2 19.4 %fusion.60 = (f32[16,2304,191]{1,2,0:T(8,128)}, f32[16,2304,191]{1,2,0:T(8,128)}) fusion(bf16[16,2688,192]{1,2,0:T(8,128)(2,1)S(1)} %copy-done), kind=kLoop, calls=%fused_computation.91 | loop fusion | bytes 112656384 | tf_op jit(solution)/shard_map/jit(_roll_static)/slice | solution.py:54
  243.7 100.3 %all-reduce.4.cloned.1.call-done = (bf16[8,2304,192]{1,2,0:T(8,128)(2,1)}, bf16[8,2304,192]{1,2,0:T(8,128)(2,1)}) async-done(((bf16[8,2304,192]{1,2,0:T(8,128)(2,1)}, bf16[8,2304,192]{1,2,0:T(8,128)(2,1)}), (bf16[8,2304,192]{1,2,0:T(8,128)(2,1)}, bf16[8,2304,192]{1,2,0:T(8,128)(2,1)})) %all-reduce.4.cloned.1.call-update) | async-done | bytes 14155792 | tf_op jit(solution)/shard_map/psum | solution.py:21
  362.6 27.7 %fusion.42 = (f32[8,2]{1,0:T(8,128)S(1)}, f32[8,2]{1,0:T(8,128)S(1)}, f32[8,2,2304,192]{2,3,1,0:T(8,128)}, f32[8,2,2304,192]{2,3,1,0:T(8,128)}) fusion(f32[2,2304,192]{1,2,0:T(8,128)S(1)} %copy-done.7, f32[8,2304,192]{1,2,0:T(8,128)} %convert_element_type.41, f32[8,2304,192]{1,2,0:T(8,128)} %convert_element_type.47), kind=kLoop, calls=%fused_computation.69 | loop fusion | flops 28311520 | bytes 88473728 | tf_op jit(solution)/shard_map/reduce_sum | solution.py:65
  390.2 30.2 %all-reduce = (f32[8,2]{1,0:T(8,128)S(1)}, f32[8,2]{1,0:T(8,128)S(1)}) all-reduce(f32[8,2]{1,0:T(8,128)S(1)} %get-tuple-element.6, f32[8,2]{1,0:T(8,128)S(1)} %get-tuple-element.5), channel_id=1, replica_groups=mesh['band'=2,'domain'=16] {'domain'}, use_global_device_ids=true, to_apply=%region_6.7 | all-reduce | flops 32 | bytes 256 | tf_op jit(solution)/shard_map/psum | solution.py:92
  420.6 97.4 %fusion.38 = bf16[16,2304,192]{1,2,0:T(8,128)(2,1)} fusion(f32[16,2688,192]{1,2,0:T(8,128)} %convert_element_type.40, f32[16,2304,191]{1,2,0:T(8,128)} %get-tuple-element.26, f32[16,2304,1]{1,2,0:T(1,128)} %get-tuple-element.28, f32[16,2304,1]{1,2,0:T(1,128)} %get-tuple-element.27, f32[16,2304,191]{1,2,0:T(8,128)} %get-tuple-element.25, ...), kind=kLoop, calls=%fused_computation.54 | loop fusion | flops 99090432 | bytes 268964416 | tf_op jit(solution)/shard_map/convert_element_type | solution.py:76
  526.8 85.2 %fusion.18 = bf16[16,2304,192]{1,2,0:T(8,128)(2,1)} fusion(f32[16,2688,192]{1,2,0:T(8,128)} %convert_element_type.46, f32[16,2304,191]{1,2,0:T(8,128)} %get-tuple-element.38, f32[16,2304,1]{1,2,0:T(1,128)S(1)} %copy-done.9, f32[16,2304,1]{1,2,0:T(1,128)S(1)} %copy-done.8, f32[16,2304,191]{1,2,0:T(8,128)} %get-tuple-element.37, ...), kind=kLoop, calls=%fused_computation.25 | loop fusion | flops 99090432 | bytes 268964416 | tf_op jit(solution)/shard_map/convert_element_type | solution.py:76
  621.3 29.3 %concatenate.59 = bf16[16,2688,192]{1,2,0:T(8,128)(2,1)} concatenate(bf16[16,192,192]{1,2,0:T(8,128)(2,1)S(1)} %collective-permute-done.2, bf16[16,2304,192]{1,2,0:T(8,128)(2,1)} %fusion.38, bf16[16,192,192]{1,2,0:T(8,128)(2,1)S(1)} %collective-permute-done.3), dimensions={1} | concatenate | bytes 33030144 | tf_op jit(solution)/shard_map/concatenate | solution.py:34
  650.5 33.1 %fusion.52 = (f32[16,2304,191]{1,2,0:T(8,128)}, f32[16,2304,191]{1,2,0:T(8,128)}) fusion(bf16[16,2688,192]{1,2,0:T(8,128)(2,1)} %concatenate.59), kind=kLoop, calls=%fused_computation.83 | loop fusion | bytes 112656384 | tf_op jit(solution)/shard_map/jit(_roll_static)/slice | solution.py:54
  696.3 29.7 %concatenate.68 = bf16[16,2688,192]{1,2,0:T(8,128)(2,1)} concatenate(bf16[16,192,192]{1,2,0:T(8,128)(2,1)} %collective-permute-done.8, bf16[16,2304,192]{1,2,0:T(8,128)(2,1)} %fusion.18, bf16[16,192,192]{1,2,0:T(8,128)(2,1)} %collective-permute-done.9), dimensions={1} | concatenate | bytes 33030144 | tf_op jit(solution)/shard_map/concatenate | solution.py:34
  726.1 33.1 %fusion.58 = (f32[16,2304,191]{1,2,0:T(8,128)}, f32[16,2304,191]{1,2,0:T(8,128)}) fusion(bf16[16,2688,192]{1,2,0:T(8,128)(2,1)} %concatenate.68), kind=kLoop, calls=%fused_computation.89 | loop fusion | bytes 112656384 | tf_op jit(solution)/shard_map/jit(_roll_static)/slice | solution.py:54
  771.9 85.2 %fusion.31 = bf16[16,2304,192]{1,2,0:T(8,128)(2,1)} fusion(f32[16,2688,192]{1,2,0:T(8,128)} %convert_element_type.43, f32[16,2304,191]{1,2,0:T(8,128)} %get-tuple-element.22, f32[16,2304,1]{1,2,0:T(1,128)S(1)} %get-tuple-element.24, f32[16,2304,1]{1,2,0:T(1,128)S(1)} %get-tuple-element.23, f32[16,2304,191]{1,2,0:T(8,128)} %get-tuple-element.21, ...), kind=kLoop, calls=%fused_computation.44 | loop fusion | flops 99090432 | bytes 268964416 | tf_op jit(solution)/shard_map/convert_element_type | solution.py:76
  864.6 85.2 %fusion.11 = bf16[16,2304,192]{1,2,0:T(8,128)(2,1)} fusion(f32[16,2688,192]{1,2,0:T(8,128)} %convert_element_type.49, f32[16,2304,191]{1,2,0:T(8,128)} %get-tuple-element.34, f32[16,2304,1]{1,2,0:T(1,128)S(1)} %get-tuple-element.36, f32[16,2304,1]{1,2,0:T(1,128)S(1)} %get-tuple-element.35, f32[16,2304,191]{1,2,0:T(8,128)} %get-tuple-element.33, ...), kind=kLoop, calls=%fused_computation.15 | loop fusion | flops 99090432 | bytes 268964416 | tf_op jit(solution)/shard_map/convert_element_type | solution.py:76
  958.5 29.3 %concatenate.62 = bf16[16,2688,192]{1,2,0:T(8,128)(2,1)} concatenate(bf16[16,192,192]{1,2,0:T(8,128)(2,1)S(1)} %collective-permute-done.4, bf16[16,2304,192]{1,2,0:T(8,128)(2,1)} %fusion.31, bf16[16,192,192]{1,2,0:T(8,128)(2,1)} %collective-permute-done.5), dimensions={1} | concatenate | bytes 33030144 | tf_op jit(solution)/shard_map/concatenate | solution.py:34
  987.9 33.1 %fusion.50 = (f32[16,2304,191]{1,2,0:T(8,128)}, f32[16,2304,191]{1,2,0:T(8,128)}) fusion(bf16[16,2688,192]{1,2,0:T(8,128)(2,1)} %concatenate.62), kind=kLoop, calls=%fused_computation.81 | loop fusion | bytes 112656384 | tf_op jit(solution)/shard_map/jit(_roll_static)/slice | solution.py:54
  1033.7 29.4 %concatenate.71 = bf16[16,2688,192]{1,2,0:T(8,128)(2,1)} concatenate(bf16[16,192,192]{1,2,0:T(8,128)(2,1)S(1)} %collective-permute-done.10, bf16[16,2304,192]{1,2,0:T(8,128)(2,1)} %fusion.11, bf16[16,192,192]{1,2,0:T(8,128)(2,1)} %collective-permute-done.11), dimensions={1} | concatenate | bytes 33030144 | tf_op jit(solution)/shard_map/concatenate | solution.py:34
  1063.0 33.1 %fusion.56 = (f32[16,2304,191]{1,2,0:T(8,128)}, f32[16,2304,191]{1,2,0:T(8,128)}) fusion(bf16[16,2688,192]{1,2,0:T(8,128)(2,1)} %concatenate.71), kind=kLoop, calls=%fused_computation.87 | loop fusion | bytes 112656384 | tf_op jit(solution)/shard_map/jit(_roll_static)/slice | solution.py:54
  1108.8 90.2 %fusion.24 = f32[16,2304,192]{1,2,0:T(8,128)} fusion(f32[16,2688,192]{1,2,0:T(8,128)} %convert_element_type.45, f32[16,2304,191]{1,2,0:T(8,128)} %get-tuple-element.18, f32[16,2304,1]{1,2,0:T(1,128)S(1)} %get-tuple-element.20, f32[16,2304,1]{1,2,0:T(1,128)S(1)} %get-tuple-element.19, f32[16,2304,191]{1,2,0:T(8,128)} %get-tuple-element.17, ...), kind=kLoop, calls=%fused_computation.34 | loop fusion | flops 92012544 | bytes 283120192 | tf_op jit(solution)/shard_map/div | solution.py:55
  1213.1 90.4 %fusion.4 = f32[16,2304,192]{1,2,0:T(8,128)} fusion(f32[16,2688,192]{1,2,0:T(8,128)} %convert_element_type.51, f32[16,2304,191]{1,2,0:T(8,128)} %get-tuple-element.30, f32[16,2304,1]{1,2,0:T(1,128)S(1)} %get-tuple-element.32, f32[16,2304,1]{1,2,0:T(1,128)S(1)} %get-tuple-element.31, f32[16,2304,191]{1,2,0:T(8,128)} %get-tuple-element.29, ...), kind=kLoop, calls=%fused_computation.5 | loop fusion | flops 92012544 | bytes 283120192 | tf_op jit(solution)/shard_map/div | solution.py:55
  (86 shorter events, 180.1 us)
Async XLA Ops:
  6.5 337.5 %all-reduce.4.cloned.1.call-start = ((), (), s32[]{:S(2)}) async-start(), calls=%async_computation | async-start | bytes 28311552 | tf_op jit(solution)/shard_map/psum | solution.py:21
  33.7 53.8 %collective-permute-start = (bf16[16,192,192]{1,2,0:T(8,128)(2,1)}, bf16[16,192,192]{1,2,0:T(8,128)(2,1)S(1)}, u32[]{:S(2)}, u32[]{:S(2)}) collective-permute-start(bf16[16,192,192]{1,2,0:T(8,128)(2,1)} %get-tuple-element.46), channel_id=1, source_target_pairs={{0,1},{1,2},{2,3},{3,4},{4,5},{5,6},{6,7},{7,8},{8,9},{9,10},{10,1... | collective-permute-start | bytes 3538952 | tf_op jit(solution)/shard_map/ppermute | solution.py:30
  36.1 54.2 %collective-permute-start.1 = (bf16[16,192,192]{1,2,0:T(8,128)(2,1)}, bf16[16,192,192]{1,2,0:T(8,128)(2,1)}, u32[]{:S(2)}, u32[]{:S(2)}) collective-permute-start(bf16[16,192,192]{1,2,0:T(8,128)(2,1)} %get-tuple-element.45), channel_id=1, source_target_pairs={{1,0},{2,1},{3,2},{4,3},{5,4},{6,5},{7,6},{8,7},{9,8},{10,9},{11,1... | collective-permute-start | bytes 3538952 | tf_op jit(solution)/shard_map/ppermute | solution.py:33
  42.4 95.8 %collective-permute-start.6 = (bf16[16,192,192]{1,2,0:T(8,128)(2,1)}, bf16[16,192,192]{1,2,0:T(8,128)(2,1)S(1)}, u32[]{:S(2)}, u32[]{:S(2)}) collective-permute-start(bf16[16,192,192]{1,2,0:T(8,128)(2,1)} %get-tuple-element.52), channel_id=1, source_target_pairs={{0,1},{1,2},{2,3},{3,4},{4,5},{5,6},{6,7},{7,8},{8,9},{9,10},{10,1... | collective-permute-start | bytes 3538952 | tf_op jit(solution)/shard_map/ppermute | solution.py:30
  44.8 93.4 %collective-permute-start.7 = (bf16[16,192,192]{1,2,0:T(8,128)(2,1)}, bf16[16,192,192]{1,2,0:T(8,128)(2,1)}, u32[]{:S(2)}, u32[]{:S(2)}) collective-permute-start(bf16[16,192,192]{1,2,0:T(8,128)(2,1)} %get-tuple-element.51), channel_id=1, source_target_pairs={{1,0},{2,1},{3,2},{4,3},{5,4},{6,5},{7,6},{8,7},{9,8},{10,9},{11,1... | collective-permute-start | bytes 3538952 | tf_op jit(solution)/shard_map/ppermute | solution.py:33
  167.6 23.9 %copy-start = (bf16[16,2688,192]{1,2,0:T(8,128)(2,1)S(1)}, bf16[16,2688,192]{1,2,0:T(8,128)(2,1)}, u32[]{:S(2)}) copy-start(bf16[16,2688,192]{1,2,0:T(8,128)(2,1)} %concatenate.65) | copy-start | bytes 49545220
  243.7 118.9 %copy-start.7 = (f32[2,2304,192]{1,2,0:T(8,128)S(1)}, f32[2,2304,192]{1,2,0:T(8,128)}, u32[]{:S(2)}) copy-start(f32[2,2304,192]{1,2,0:T(8,128)} %param.4) | copy-start | bytes 10616836
  420.6 97.4 %copy-start.10 = (f32[16]{0:T(128)}, f32[16]{0:T(128)S(1)}, u32[]{:S(2)}) copy-start(f32[16]{0:T(128)S(1)} %sub.26) | copy-start | bytes 196
  420.6 106.2 %copy-start.8 = (f32[16,2304,1]{1,2,0:T(1,128)S(1)}, f32[16,2304,1]{1,2,0:T(1,128)}, u32[]{:S(2)}) copy-start(f32[16,2304,1]{1,2,0:T(1,128)} %get-tuple-element.39) | copy-start | bytes 442372
  420.6 106.2 %copy-start.9 = (f32[16,2304,1]{1,2,0:T(1,128)S(1)}, f32[16,2304,1]{1,2,0:T(1,128)}, u32[]{:S(2)}) copy-start(f32[16,2304,1]{1,2,0:T(1,128)} %get-tuple-element.40) | copy-start | bytes 442372
  522.3 99.0 %collective-permute-start.2 = (bf16[16,192,192]{1,2,0:T(8,128)(2,1)}, bf16[16,192,192]{1,2,0:T(8,128)(2,1)S(1)}, u32[]{:S(2)}, u32[]{:S(2)}) collective-permute-start(bf16[16,192,192]{1,2,0:T(8,128)(2,1)} %get-tuple-element.44), channel_id=1, source_target_pairs={{0,1},{1,2},{2,3},{3,4},{4,5},{5,6},{6,7},{7,8},{8,9},{9,10},{10,1... | collective-permute-start | bytes 3538952 | tf_op jit(solution)/shard_map/ppermute | solution.py:30
  523.3 98.0 %collective-permute-start.3 = (bf16[16,192,192]{1,2,0:T(8,128)(2,1)}, bf16[16,192,192]{1,2,0:T(8,128)(2,1)S(1)}, u32[]{:S(2)}, u32[]{:S(2)}) collective-permute-start(bf16[16,192,192]{1,2,0:T(8,128)(2,1)} %get-tuple-element.43), channel_id=1, source_target_pairs={{1,0},{2,1},{3,2},{4,3},{5,4},{6,5},{7,6},{8,7},{9,8},{10,9},{11,1... | collective-permute-start | bytes 3538952 | tf_op jit(solution)/shard_map/ppermute | solution.py:33
  526.7 85.2 %copy-start.13 = (f32[16]{0:T(128)}, f32[16]{0:T(128)S(1)}, u32[]{:S(2)}) copy-start(f32[16]{0:T(128)S(1)} %sub.30) | copy-start | bytes 196
  616.4 79.9 %collective-permute-start.8 = (bf16[16,192,192]{1,2,0:T(8,128)(2,1)}, bf16[16,192,192]{1,2,0:T(8,128)(2,1)}, u32[]{:S(2)}, u32[]{:S(2)}) collective-permute-start(bf16[16,192,192]{1,2,0:T(8,128)(2,1)} %get-tuple-element.50), channel_id=1, source_target_pairs={{0,1},{1,2},{2,3},{3,4},{4,5},{5,6},{6,7},{7,8},{8,9},{9,10},{10,1... | collective-permute-start | bytes 3538952 | tf_op jit(solution)/shard_map/ppermute | solution.py:30
  616.4 80.0 %collective-permute-start.9 = (bf16[16,192,192]{1,2,0:T(8,128)(2,1)}, bf16[16,192,192]{1,2,0:T(8,128)(2,1)}, u32[]{:S(2)}, u32[]{:S(2)}) collective-permute-start(bf16[16,192,192]{1,2,0:T(8,128)(2,1)} %get-tuple-element.49), channel_id=1, source_target_pairs={{1,0},{2,1},{3,2},{4,3},{5,4},{6,5},{7,6},{8,7},{9,8},{10,9},{11,1... | collective-permute-start | bytes 3538952 | tf_op jit(solution)/shard_map/ppermute | solution.py:33
  650.5 34.5 %copy-start.1 = (bf16[16,2688,192]{1,2,0:T(8,128)(2,1)S(1)}, bf16[16,2688,192]{1,2,0:T(8,128)(2,1)}, u32[]{:S(2)}) copy-start(bf16[16,2688,192]{1,2,0:T(8,128)(2,1)} %concatenate.59) | copy-start | bytes 49545220
  726.1 34.5 %copy-start.2 = (bf16[16,2688,192]{1,2,0:T(8,128)(2,1)S(1)}, bf16[16,2688,192]{1,2,0:T(8,128)(2,1)}, u32[]{:S(2)}) copy-start(bf16[16,2688,192]{1,2,0:T(8,128)(2,1)} %concatenate.68) | copy-start | bytes 49545220
  771.9 92.7 %copy-start.14 = (f32[16]{0:T(128)S(1)}, f32[16]{0:T(128)}, u32[]{:S(2)}) copy-start(f32[16]{0:T(128)} %copy-done.13) | copy-start | bytes 196
  859.8 98.7 %collective-permute-start.4 = (bf16[16,192,192]{1,2,0:T(8,128)(2,1)S(1)}, bf16[16,192,192]{1,2,0:T(8,128)(2,1)S(1)}, u32[]{:S(2)}, u32[]{:S(2)}) collective-permute-start(bf16[16,192,192]{1,2,0:T(8,128)(2,1)S(1)} %get-tuple-element.42), channel_id=1, source_target_pairs={{0,1},{1,2},{2,3},{3,4},{4,5},{5,6},{6,7},{7,8},{8,9},{9,10},{10,1... | collective-permute-start | bytes 3538952 | tf_op jit(solution)/shard_map/ppermute | solution.py:30
  859.9 98.6 %collective-permute-start.5 = (bf16[16,192,192]{1,2,0:T(8,128)(2,1)S(1)}, bf16[16,192,192]{1,2,0:T(8,128)(2,1)}, u32[]{:S(2)}, u32[]{:S(2)}) collective-permute-start(bf16[16,192,192]{1,2,0:T(8,128)(2,1)S(1)} %get-tuple-element.41), channel_id=1, source_target_pairs={{1,0},{2,1},{3,2},{4,3},{5,4},{6,5},{7,6},{8,7},{9,8},{10,9},{11,1... | collective-permute-start | bytes 3538952 | tf_op jit(solution)/shard_map/ppermute | solution.py:33
  954.2 79.5 %collective-permute-start.10 = (bf16[16,192,192]{1,2,0:T(8,128)(2,1)}, bf16[16,192,192]{1,2,0:T(8,128)(2,1)S(1)}, u32[]{:S(2)}, u32[]{:S(2)}) collective-permute-start(bf16[16,192,192]{1,2,0:T(8,128)(2,1)} %get-tuple-element.48), channel_id=1, source_target_pairs={{0,1},{1,2},{2,3},{3,4},{4,5},{5,6},{6,7},{7,8},{8,9},{9,10},{10,1... | collective-permute-start | bytes 3538952 | tf_op jit(solution)/shard_map/ppermute | solution.py:30
  954.2 79.5 %collective-permute-start.11 = (bf16[16,192,192]{1,2,0:T(8,128)(2,1)}, bf16[16,192,192]{1,2,0:T(8,128)(2,1)}, u32[]{:S(2)}, u32[]{:S(2)}) collective-permute-start(bf16[16,192,192]{1,2,0:T(8,128)(2,1)} %get-tuple-element.47), channel_id=1, source_target_pairs={{1,0},{2,1},{3,2},{4,3},{5,4},{6,5},{7,6},{8,7},{9,8},{10,9},{11,1... | collective-permute-start | bytes 3538952 | tf_op jit(solution)/shard_map/ppermute | solution.py:33
  987.9 34.5 %copy-start.3 = (bf16[16,2688,192]{1,2,0:T(8,128)(2,1)S(1)}, bf16[16,2688,192]{1,2,0:T(8,128)(2,1)}, u32[]{:S(2)}) copy-start(bf16[16,2688,192]{1,2,0:T(8,128)(2,1)} %concatenate.62) | copy-start | bytes 49545220
  1063.0 34.5 %copy-start.4 = (bf16[16,2688,192]{1,2,0:T(8,128)(2,1)S(1)}, bf16[16,2688,192]{1,2,0:T(8,128)(2,1)}, u32[]{:S(2)}) copy-start(bf16[16,2688,192]{1,2,0:T(8,128)(2,1)} %concatenate.71) | copy-start | bytes 49545220
  (5 other events, 54.2 us)
Sparse Core Ops, SparseCore 0:
  19.3 324.6 all-reduce.3
where the time goes:
time: 1340 us; the launch traced here: 1330 us
  other arithmetic  701 us (52%)
  local copies, waits for them, and re-layouts  412 us (31%)
  waiting for transfers between devices  146 us (11%)
  blocking collectives  30.2 us (2%)
  starting transfers between devices  23.2 us (2%)
  between operations  15.1 us (1%)
    convert_element_type x4, other arithmetic, solve_block(): potential.astype(jnp.bfloat16)  353 us
    slice x12, local copies, waits for them, and re-layouts, row_sweep(): jnp.roll(centre, -1, 2)  190 us
    div x2, other arithmetic, row_sweep(): return (beside + coupling * source) / 6.0  181 us
    concatenate x6, local copies, waits for them, and re-layouts, padded(): block = jnp.concatenate([low, block, high], axis=dim)  177 us
    psum x1, waiting for transfers between devices, spread(): return lax.psum(block, axis)  100 us
    convert_element_type x6, other arithmetic, solve_block(): padded(potential.astype(jnp.bfloat16), (('domain', 1),), GY)  80.7 us
    ppermute x6, waiting for transfers between devices, padded(): lax.ppermute(lax.slice_in_dim(block, block.shape[dim] - width, None, axis...  42.7 us
    psum x1, blocking collectives, body(): totals = lax.psum(local_sums, 'domain')  30.2 us
  transfers between devices with their start and end apart: 13, of which 3 were waited for; matrix products, arithmetic and copies ran while one was open for 37% of the time, Pallas kernels for 0%

commit v1 on v0

--- a/solution.py
+++ b/solution.py
@@ -1,8 +1,11 @@
+import functools
 import math
 
 import jax
 import jax.numpy as jnp
 from jax import lax
+from jax.experimental import pallas as pl
+from jax.experimental.pallas import tpu as pltpu
 from jax.sharding import PartitionSpec as P
 
 ORB = 8
@@ -81,7 +84,7 @@
     return jnp.sum(potential * partner[:, None], axis=0)
 
 
-def body(targets, partner_pool, owners, warm_start):
+def sweep_body(targets, partner_pool, owners, warm_start):
     row_count = targets.shape[1]
     first_row = lax.axis_index("domain") * row_count
     cell_count = GX * GY * GZ
@@ -94,6 +97,305 @@
             partner, density, totals / cell_count, warm_start[block_index], first_row
         )
     return exchange
+
+
+EDGE = SWEEPS
+
+
+def coupled(centre, ring):
+    return jnp.dot(ring, centre, preferred_element_type=jnp.float32) + jnp.dot(
+        centre, ring, preferred_element_type=jnp.float32
+    )
+
+
+def sums_kernel(planes, low_ref, mid_ref, high_ref, targets_ref, sums_ref):
+    mid = planes - 2 * EDGE
+
+    def add(piece, index, plane, totals):
+        partner = piece[0, index].astype(jnp.float32)
+        return tuple(
+            total + jnp.sum((partner * targets_ref[j, plane]).reshape(-1, 8, GZ), axis=0)
+            for j, total in enumerate(totals)
+        )
+
+    totals = tuple(jnp.zeros((8, GZ), jnp.float32) for _ in range(targets_ref.shape[0]))
+    totals = lax.fori_loop(0, EDGE, lambda k, t: add(low_ref, k, k, t), totals)
+    totals = lax.fori_loop(0, mid, lambda k, t: add(mid_ref, k, k + EDGE, t), totals)
+    totals = lax.fori_loop(0, EDGE, lambda k, t: add(high_ref, k, k + EDGE + mid, t), totals)
+    for j, total in enumerate(totals):
+        sums_ref[0, j] = total
+
+
+def pair_sums(pieces, targets):
+    count, planes = targets.shape[:2]
+    out = pl.pallas_call(
+        functools.partial(sums_kernel, planes),
+        grid=(ORB,),
+        in_specs=[
+            pl.BlockSpec((1,) + piece.shape[1:], lambda i: (i, 0, 0, 0)) for piece in pieces
+        ]
+        + [pl.BlockSpec(targets.shape, lambda i: (0, 0, 0, 0), pipeline_mode=pl.Buffered(1))],
+        out_specs=pl.BlockSpec((1, count, 8, GZ), lambda i: (i, 0, 0, 0)),
+        out_shape=jax.ShapeDtypeStruct((ORB, count, 8, GZ), jnp.float32),
+        cost_estimate=pl.CostEstimate(
+            flops=2 * ORB * targets.size, bytes_accessed=11_000_000, transcendentals=0
+        ),
+        compiler_params=pltpu.CompilerParams(vmem_limit_bytes=40 << 20),
+    )(*pieces, targets)
+    return jnp.sum(out, axis=(2, 3))
+
+
+def window_kernel(
+    planes,
+    step_ref,
+    below_ref,
+    low_ref,
+    mid_ref,
+    high_ref,
+    above_ref,
+    targets_ref,
+    warm_ref,
+    ring_ref,
+    out_ref,
+    partner,
+    target,
+    start,
+    first,
+    second,
+):
+    i, j = pl.program_id(0), pl.program_id(1)
+    mid = planes - 2 * EDGE
+    wide = planes + 2 * EDGE
+    blank = jnp.zeros((GY, GZ), jnp.float32)
+
+    @pl.when((i == 0) & (j == 0))
+    def _():
+        for t in range(targets_ref.shape[0]):
+            for e in range(EDGE):
+                target[t, e] = blank
+                target[t, planes + EDGE + e] = blank
+
+            def place(k, carry, t=t):
+                target[t, k + EDGE] = targets_ref[t, k]
+                return carry
+
+            lax.fori_loop(0, planes, place, 0)
+
+        def clear(k, carry):
+            for t in range(targets_ref.shape[0]):
+                out_ref[t, k] = blank
+            return carry
+
+        lax.fori_loop(0, wide, clear, 0)
+        for e in range(EDGE + 1):
+            start[e] = blank.astype(start.dtype)
+            start[planes + EDGE + 1 + e] = blank.astype(start.dtype)
+            first[e] = blank
+            first[planes + EDGE + 1 + e] = blank
+            second[e] = blank
+            second[planes + EDGE + 1 + e] = blank
+
+    @pl.when(j == 0)
+    def _():
+        place_at = 0
+        for piece in (below_ref, low_ref, mid_ref, high_ref, above_ref):
+
+            def place(k, carry, piece=piece, place_at=place_at):
+                partner[place_at + k] = piece[0, k].astype(jnp.float32)
+                return carry
+
+            lax.fori_loop(0, piece.shape[1], place, 0)
+            place_at += piece.shape[1]
+
+    def load(k, carry):
+        start[k + EDGE + 1] = warm_ref[0, 0, 0, k]
+        return carry
+
+    lax.fori_loop(0, planes, load, 0)
+    ring = ring_ref[...]
+
+    def swept(field, e, weight):
+        centre = field[e + 1]
+        beside = field[e].astype(jnp.float32) + field[e + 2].astype(jnp.float32)
+        source = (partner[e] * weight) * target[j, e]
+        return beside + source + coupled(centre.astype(jnp.bfloat16), ring)
+
+    def sweep_one(n, carry):
+        for half in range(2):
+            e = 2 + 2 * n + half
+            first[e + 1] = swept(start, e, coupling)
+        return carry
+
+    def sweep_two(n, carry):
+        for half in range(2):
+            e = 1 + 2 * n + half
+            second[e + 1] = swept(first, e, 6.0 * coupling)
+        return carry
+
+    def sweep_three(n, carry):
+        for half in range(2):
+            e = 2 * n + half
+            out_ref[j, e] += swept(second, e, 36.0 * coupling) * (partner[e] * (-1.0 / 216.0))
+        return carry
+
+    lax.fori_loop(0, (planes + 2) // 2, sweep_one, 0)
+    lax.fori_loop(0, (planes + 4) // 2, sweep_two, 0)
+    lax.fori_loop(0, (planes + 6) // 2, sweep_three, 0)
+
+
+def window(step, below, pieces, above, targets, warm_start, ring):
+    count, planes = targets.shape[:2]
+    wide = planes + 2 * EDGE
+    parts = (below,) + tuple(pieces) + (above,)
+    plane = (GY, GZ)
+    grid_spec = pltpu.PrefetchScalarGridSpec(
+        num_scalar_prefetch=1,
+        grid=(ORB, count),
+        in_specs=[
+            pl.BlockSpec((1,) + part.shape[1:], lambda i, j, s: (i, 0, 0, 0)) for part in parts
+        ]
+        + [
+            pl.BlockSpec(targets.shape, lambda i, j, s: (0, 0, 0, 0), pipeline_mode=pl.Buffered(1)),
+            pl.BlockSpec((1, 1, 1, planes) + plane, lambda i, j, s: (s[0], i, j, 0, 0, 0)),
+            pl.BlockSpec(plane, lambda i, j, s: (0, 0), pipeline_mode=pl.Buffered(1)),
+        ],
+        out_specs=pl.BlockSpec((count, wide) + plane, lambda i, j, s: (0, 0, 0, 0), pipeline_mode=pl.Buffered(1)),
+        scratch_shapes=[
+            pltpu.VMEM((wide,) + plane, jnp.float32),
+            pltpu.VMEM((count, wide) + plane, jnp.float32),
+            pltpu.VMEM((wide + 2,) + plane, jnp.bfloat16),
+            pltpu.VMEM((wide + 2,) + plane, jnp.float32),
+            pltpu.VMEM((wide + 2,) + plane, jnp.float32),
+        ],
+    )
+    return pl.pallas_call(
+        functools.partial(window_kernel, planes),
+        grid_spec=grid_spec,
+        out_shape=jax.ShapeDtypeStruct((count, wide) + plane, jnp.float32),
+        cost_estimate=pl.CostEstimate(
+            flops=ORB * count * 48 * 4 * GY * GY * GZ, bytes_accessed=30_000_000, transcendentals=0
+        ),
+        compiler_params=pltpu.CompilerParams(vmem_limit_bytes=56 << 20),
+    )(step.reshape(1), *parts, targets, warm_start, ring)
+
+
+def final_kernel(planes, means_ref, *refs):
+    own, remote, own_low, own_high, remote_low, remote_high = refs[:6]
+    pieces = (refs[6:9], refs[9:12])
+    out_ref = refs[12]
+    k = pl.program_id(0)
+    count = out_ref.shape[0]
+    for j in range(count):
+        out_ref[j, 0] = own[j, 0] + remote[j, 0]
+
+    def constants(which):
+        for j in range(count):
+            total = out_ref[j, 0]
+            for block in range(2):
+                for i in range(ORB):
+                    total += means_ref[block * ORB + i, j] * pieces[block][which][i, 0].astype(
+                        jnp.float32
+                    )
+            out_ref[j, 0] = total
+
+    @pl.when(k < EDGE)
+    def _():
+        for j in range(count):
+            out_ref[j, 0] += own_low[j, 0] + remote_low[j, 0]
+        constants(0)
+
+    @pl.when((k >= EDGE) & (k < planes - EDGE))
+    def _():
+        constants(1)
+
+    @pl.when(k >= planes - EDGE)
+    def _():
+        for j in range(count):
+            out_ref[j, 0] += own_high[j, 0] + remote_high[j, 0]
+        constants(2)
+
+
+def final_sum(means, own, remote, sides, own_pieces, remote_pieces):
+    count, wide = own.shape[:2]
+    planes = wide - 2 * EDGE
+    plane = (GY, GZ)
+    mid = planes - 2 * EDGE
+    at_low = lambda k: (0, jnp.minimum(k, EDGE - 1), 0, 0)
+    at_mid = lambda k: (0, jnp.clip(k - EDGE, 0, mid - 1), 0, 0)
+    at_high = lambda k: (0, jnp.maximum(k - (planes - EDGE), 0), 0, 0)
+    centre = pl.BlockSpec((count, 1) + plane, lambda k: (0, k + EDGE, 0, 0))
+    side = [pl.BlockSpec((count, 1) + plane, at) for at in (at_low, at_high)]
+    piece = [pl.BlockSpec((ORB, 1) + plane, at) for at in (at_low, at_mid, at_high)]
+    return pl.pallas_call(
+        functools.partial(final_kernel, planes),
+        grid=(planes,),
+        in_specs=[pl.BlockSpec(memory_space=pltpu.SMEM), centre, centre] + side + side + piece + piece,
+        out_specs=pl.BlockSpec((count, 1) + plane, lambda k: (0, k, 0, 0)),
+        out_shape=jax.ShapeDtypeStruct((count, planes) + plane, jnp.float32),
+        cost_estimate=pl.CostEstimate(
+            flops=40 * count * planes * GY * GZ, bytes_accessed=28_000_000, transcendentals=0
+        ),
+        compiler_params=pltpu.CompilerParams(vmem_limit_bytes=40 << 20),
+    )(means, own, remote, *sides, *own_pieces, *remote_pieces)
+
+
+def plane_body(targets, partner_pool, owners, warm_start):
+    count, rows = targets.shape[:2]
+    planes = rows // GY
+    plane = (GY, GZ)
+    targets = targets.reshape((count, planes) + plane)
+    pool = partner_pool.reshape((partner_pool.shape[0], planes) + plane)
+    warm = warm_start.reshape((STEPS, ORB, count, planes) + plane)
+    devices = lax.axis_size("domain")
+    upward = [(d, (d + 1) % devices) for d in range(devices)]
+    downward = [(d, (d - 1) % devices) for d in range(devices)]
+    swap = [(0, 1), (1, 0)]
+    band = lax.axis_index("band")
+    own_step = jnp.where(owners[0] == band, 0, 1).astype(jnp.int32)
+    mid = planes - 2 * EDGE
+
+    def cut(at, size):
+        return lax.dynamic_slice(pool, (own_step * ORB, at, 0, 0), (ORB, size) + plane)
+
+    own_pieces = (cut(0, EDGE), cut(EDGE, mid), cut(planes - EDGE, EDGE))
+    low, middle, high = own_pieces
+    far_low = lax.ppermute(low, "band", swap)
+    far_high = lax.ppermute(high, "band", swap)
+    far_mid = lax.ppermute(middle, "band", swap)
+    far_pieces = (far_low, far_mid, far_high)
+    below = lax.ppermute(high, "domain", upward)
+    above = lax.ppermute(low, "domain", downward)
+    far_below = lax.ppermute(far_high, "domain", upward)
+    far_above = lax.ppermute(far_low, "domain", downward)
+
+    index = jnp.arange(GY, dtype=jnp.int32)
+    apart = (index[:, None] - index[None, :]) % GY
+    ring = ((apart == 1) | (apart == GY - 1)).astype(jnp.bfloat16)
+
+    def sent(field):
+        to_above = lax.ppermute(field[:, planes + EDGE :], "domain", upward)
+        to_below = lax.ppermute(field[:, :EDGE], "domain", downward)
+        return (to_above, to_below)
+
+    own_sums = pair_sums(own_pieces, targets)
+    own = window(own_step, below, own_pieces, above, targets, warm, ring)
+    own_sides = sent(own)
+    far_sums = pair_sums(far_pieces, targets)
+    totals = lax.psum(jnp.concatenate([own_sums, far_sums], axis=0), "domain")
+    means = totals * (coupling / (2.0 * GX * GY * GZ))
+    far = window(1 - own_step, far_below, far_pieces, far_above, targets, warm, ring)
+    far_sides = sent(far)
+    out = final_sum(means, own, far, own_sides + far_sides, own_pieces, far_pieces)
+    return out.reshape(count, rows, GZ)
+
+
+def body(targets, partner_pool, owners, warm_start):
+    rows = targets.shape[1]
+    planes = rows // GY
+    whole_planes = rows % GY == 0 and planes % 2 == 0 and planes > 2 * EDGE
+    if whole_planes and GY == GZ and lax.axis_size("band") == 2:
+        return plane_body(targets, partner_pool, owners, warm_start)
+    return sweep_body(targets, partner_pool, owners, warm_start)
 
 
 def solution(mesh):

time: 1340 us -> 485 us (0.36)
  other arithmetic: 701 us -> 2.79 us
  local copies, waits for them, and re-layouts: 412 us -> 116 us
  Pallas kernels: 0 us -> 265 us
  waiting for transfers between devices: 146 us -> 43.2 us
  between operations: 15.1 us -> 0.8 us
    convert_element_type x12 -> x1, other arithmetic: 452 us -> 0.77 us  [plane_body(): ring = ((apart == 1) | (apart == GY - 1)).astype(jnp.bfloat16)]
    pallas_call x0 -> x5, Pallas kernels: none -> 265 us  [the longest x2 230 us: window(): pl.pallas_call(functools.partial(window_kernel, planes), grid_spec=grid_s...]
    slice x20 -> x2, local copies, waits for them, and re-layouts: 225 us -> 6.6 us  [sent(): to_below = lax.ppermute(field[:, :EDGE], 'domain', downward)]
    div x4 -> x0, other arithmetic: 181 us -> none  [the longest x2 181 us: row_sweep(): return (beside + coupling * source) / 6.0]
    concatenate x6 -> x0, local copies, waits for them, and re-layouts: 177 us -> none  [padded(): block = jnp.concatenate([low, block, high], axis=dim)]
    psum x1 -> x0, waiting for transfers between devices: 100 us -> none  [spread(): return lax.psum(block, axis)]
    unnamed x32 -> x21, local copies, waits for them, and re-layouts: 10.4 us -> 94.7 us
    reduce_sum x3 -> x2, other arithmetic: 55.6 us -> 2.01 us  [pair_sums(): return jnp.sum(out, axis=(2, 3))]
  transfers between devices with their start and end apart: 13 -> 11, of which waited for: 3 -> 1; matrix products, arithmetic and copies ran while one was open for 37% -> 13% of each run, Pallas kernels for 0% -> 52%
where the time goes in v1:
time: 485 us; the launch traced here: 477 us
  Pallas kernels  265 us (55%)
  local copies, waits for them, and re-layouts  116 us (24%)
  waiting for transfers between devices  43.2 us (9%)
  blocking collectives  33.8 us (7%)
  starting transfers between devices  15.1 us (3%)
    pallas_call x2, Pallas kernels, window(): pl.pallas_call(functools.partial(window_kernel, planes), grid_spec=grid_s...  230 us
    unnamed x21, local copies, waits for them, and re-layouts  94.7 us
    ppermute x1, waiting for transfers between devices, plane_body(): far_low = lax.ppermute(low, 'band', swap)  43.2 us
    psum x1, blocking collectives, plane_body(): totals = lax.psum(jnp.concatenate([own_sums, far_sums], axis=0), 'domain')  33.8 us
    pallas_call x1, Pallas kernels, final_sum(): pl.pallas_call(functools.partial(final_kernel, planes), grid=(planes,), i...  18.7 us
    pallas_call x2, Pallas kernels, pair_sums(): pl.pallas_call(functools.partial(sums_kernel, planes), grid=(ORB,), in_sp...  16.4 us
  transfers between devices with their start and end apart: 11, of which 1 were waited for; matrix products, arithmetic and copies ran while one was open for 13% of the time, Pallas kernels for 52%

profile of v1, /device:TPU:1, one launch (start us, length us, event | category | flops | bytes accessed | tf_op | source)
XLA Modules:
  0.0 477.2 jit_solution(1407162129659810593)
XLA Ops:
  0.7 41.4 %copy.21 = bf16[32,2304,192]{2,1,0:T(8,128)(2,1)} copy(bf16[32,2304,192]{1,2,0:T(8,128)(2,1)} %param.5) | data formatting | bytes 56623104 | tf_op args[1]
  42.0 4.2 constant_dynamic-slice_fusion
  46.2 2.1 collective-permute-start.2
  48.3 2.5 collective-permute-start.3
  50.9 5.0 %constant_dynamic-slice_fusion.1.mid_ref.refs_7_ = bf16[8,6,192,192]{3,2,1,0:T(8,128)(2,1)} fusion(bf16[32,12,192,192]{3,2,1,0:T(8,128)(2,1)} %bitcast.15, s32[]{:T(128)S(6)} %select_n.19), kind=kLoop, calls=%fused_computation.12 | loop fusion | bytes 7077892 | tf_op jit(solution)/shard_map/dynamic_slice | solution.py:358
  57.1 5.5 %copy.22 = f32[2,2304,192]{2,1,0:T(8,128)} copy(f32[2,2304,192]{1,2,0:T(8,128)} %param.4) | data formatting | bytes 7077888 | tf_op args[0]
  62.6 41.4 %copy.23 = bf16[2,8,2,2304,192]{4,3,2,1,0:T(8,128)(2,1)} copy(bf16[2,8,2,2304,192]{3,4,2,1,0:T(8,128)(2,1)} %param.7) | data formatting | bytes 56623104 | tf_op args[3]
  104.8 2.0 collective-permute-start.5
  106.8 43.2 %collective-permute-done.low_ref.refs_9_ = bf16[8,3,192,192]{3,2,1,0:T(8,128)(2,1)} collective-permute-done((bf16[8,3,192,192]{3,2,1,0:T(8,128)(2,1)}, bf16[8,3,192,192]{3,2,1,0:T(8,128)(2,1)}, u32[]{:S(2)}, u32[]{:S(2)}) %collective-permute-start) | collective-permute-done | bytes 1769504 | tf_op jit(solution)/shard_map/ppermute | solution.py:362
  149.9 2.1 collective-permute-start.6
  152.0 115.1 %shard_map.48.refs_0_ = f32[2,18,192,192]{3,2,1,0:T(8,128)} custom-call(s32[1]{0:T(128)} %bitcast.3.step_ref, bf16[8,3,192,192]{3,2,1,0:T(8,128)(2,1)} %collective-permute-done.3.below_ref, bf16[8,3,192,192]{3,2,1,0:T(8,128)(2,1)} %get-tuple-element.6.low_ref.refs_6_, bf16[8,6,192,192]{3,2,1,0:T(8,128)(2,1)} %constant_dynamic-slice_fusion.1.mid_ref.refs_7_, ...), custom_call_target="tpu_custom_call" | custom-call | flops 21743271936 | bytes 30000000 | tf_op jit(solution)/shard_map/pallas_call | solution.py:271
  267.1 3.3 fusion.8
  270.4 2.5 collective-permute-start.8
  272.9 1.4 copy-done.5
  274.3 1.4 copy-done.6
  275.7 115.2 %shard_map.49.refs_1_ = f32[2,18,192,192]{3,2,1,0:T(8,128)} custom-call(s32[1]{0:T(128)} %bitcast.5.step_ref, bf16[8,3,192,192]{3,2,1,0:T(8,128)(2,1)} %copy-done.5, bf16[8,3,192,192]{3,2,1,0:T(8,128)(2,1)} %collective-permute-done.low_ref.refs_9_, bf16[8,6,192,192]{3,2,1,0:T(8,128)(2,1)} %collective-permute-done.1.mid_ref.refs_10_, ...), custom_call_target="tpu_custom_call" | custom-call | flops 21743271936 | bytes 30000000 | tf_op jit(solution)/shard_map/pallas_call | solution.py:271
  390.9 3.3 fusion.7
  394.3 2.7 collective-permute-start.10
  397.0 8.0 %shard_map.46 = f32[8,2,8,192]{3,2,1,0:T(8,128)S(1)} custom-call(bf16[8,3,192,192]{3,2,1,0:T(8,128)(2,1)} %get-tuple-element.6.low_ref.refs_6_, bf16[8,6,192,192]{3,2,1,0:T(8,128)(2,1)} %constant_dynamic-slice_fusion.1.mid_ref.refs_7_, bf16[8,3,192,192]{3,2,1,0:T(8,128)(2,1)S(1)} %copy-done.2, f32[2,12,192,192]{3,2,1,0:T(8,128)S(1)} %bitcast.12), custom_call_target="tpu_custom_call" | custom-call | flops 14155776 | bytes 11000000 | tf_op jit(solution)/shard_map/pallas_call | solution.py:131
  406.7 2.3 copy-done
  409.0 8.4 %shard_map.47 = f32[8,2,8,192]{3,2,1,0:T(8,128)S(1)} custom-call(bf16[8,3,192,192]{3,2,1,0:T(8,128)(2,1)} %collective-permute-done.low_ref.refs_9_, bf16[8,6,192,192]{3,2,1,0:T(8,128)(2,1)} %collective-permute-done.1.mid_ref.refs_10_, bf16[8,3,192,192]{3,2,1,0:T(8,128)(2,1)} %collective-permute-done.2.high_ref.refs_11_, f32[2,12,192,192]{3,2,1,0:T(8,128)S(1)} %bitcast.13), custom_call_target="tpu_custom_call" | custom-call | flops 14155776 | bytes 11000000 | tf_op jit(solution)/shard_map/pallas_call | solution.py:131
  419.1 33.8 %psum.7 = f32[16,2]{1,0:T(8,128)S(1)} all-reduce(f32[16,2]{1,0:T(8,128)S(1)} %pad_maximum_fusion), channel_id=1, replica_groups=mesh['band'=2,'domain'=16] {'domain'}, use_global_device_ids=true, to_apply=%region_2.3 | all-reduce | flops 32 | bytes 256 | tf_op jit(solution)/shard_map/psum | solution.py:384
  452.9 18.7 %shard_map.50 = f32[2,12,192,192]{3,2,1,0:T(8,128)} custom-call(f32[16,2]{1,0:T(8,128)S(1)} %broadcast_multiply_fusion.means_ref, f32[2,18,192,192]{3,2,1,0:T(8,128)} %shard_map.48.refs_0_, f32[2,18,192,192]{3,2,1,0:T(8,128)} %shard_map.49.refs_1_, f32[2,3,192,192]{3,2,1,0:T(8,128)} %collective-permute-done.7.refs_2_, ...), custom_call_target="tpu_custom_call" | custom-call | flops 35389440 | bytes 28000000 | tf_op jit(solution)/shard_map/pallas_call | solution.py:329
  471.6 5.6 %copy.24 = f32[2,2304,192]{1,2,0:T(8,128)} copy(f32[2,2304,192]{2,1,0:T(8,128)} %bitcast.18) | data formatting | bytes 7077888 | tf_op jit(solution)/shard_map/reshape | solution.py:389
  (36 shorter events, 5.4 us)
Async XLA Ops:
  46.2 9.6 %copy-start.1 = (bf16[8,3,192,192]{3,2,1,0:T(8,128)(2,1)}, bf16[8,3,192,192]{3,2,1,0:T(8,128)(2,1)S(1)}, u32[]{:S(2)}) copy-start(bf16[8,3,192,192]{3,2,1,0:T(8,128)(2,1)S(1)} %get-tuple-element.5.high_ref.refs_8_) | copy-start | bytes 5308420
  46.2 58.5 %collective-permute-start.2 = (bf16[8,3,192,192]{3,2,1,0:T(8,128)(2,1)S(1)}, bf16[8,3,192,192]{3,2,1,0:T(8,128)(2,1)}, u32[]{:S(2)}, u32[]{:S(2)}) collective-permute-start(bf16[8,3,192,192]{3,2,1,0:T(8,128)(2,1)S(1)} %get-tuple-element.5.high_ref.refs_8_), channel_id=1, source_target_pairs={{0,16},{16,0},{1,17},{17,1},{2,18},{18,2},{3,19},{19,3},{4,20},{20... | collective-permute-start | bytes 5308424 | tf_op jit(solution)/shard_map/ppermute | solution.py:363
  48.3 101.6 %collective-permute-start = (bf16[8,3,192,192]{3,2,1,0:T(8,128)(2,1)}, bf16[8,3,192,192]{3,2,1,0:T(8,128)(2,1)}, u32[]{:S(2)}, u32[]{:S(2)}) collective-permute-start(bf16[8,3,192,192]{3,2,1,0:T(8,128)(2,1)} %get-tuple-element.6.low_ref.refs_6_), channel_id=1, source_target_pairs={{0,16},{16,0},{1,17},{17,1},{2,18},{18,2},{3,19},{19,3},{4,20},{20... | collective-permute-start | bytes 5308424 | tf_op jit(solution)/shard_map/ppermute | solution.py:362
  48.3 103.7 %collective-permute-start.3 = (bf16[8,3,192,192]{3,2,1,0:T(8,128)(2,1)S(1)}, bf16[8,3,192,192]{3,2,1,0:T(8,128)(2,1)}, u32[]{:S(2)}, u32[]{:S(2)}) collective-permute-start(bf16[8,3,192,192]{3,2,1,0:T(8,128)(2,1)S(1)} %get-tuple-element.5.high_ref.refs_8_), channel_id=1, source_target_pairs={{0,1},{1,2},{2,3},{3,4},{4,5},{5,6},{6,7},{7,8},{8,9},{9,10},{10,1... | collective-permute-start | bytes 5308424 | tf_op jit(solution)/shard_map/ppermute | solution.py:366
  50.9 101.1 %collective-permute-start.4 = (bf16[8,3,192,192]{3,2,1,0:T(8,128)(2,1)}, bf16[8,3,192,192]{3,2,1,0:T(8,128)(2,1)}, u32[]{:S(2)}, u32[]{:S(2)}) collective-permute-start(bf16[8,3,192,192]{3,2,1,0:T(8,128)(2,1)} %get-tuple-element.6.low_ref.refs_6_), channel_id=1, source_target_pairs={{0,15},{1,0},{2,1},{3,2},{4,3},{5,4},{6,5},{7,6},{8,7},{9,8},{10,9... | collective-permute-start | bytes 5308424 | tf_op jit(solution)/shard_map/ppermute | solution.py:367
  55.9 219.8 %collective-permute-start.1 = (bf16[8,6,192,192]{3,2,1,0:T(8,128)(2,1)}, bf16[8,6,192,192]{3,2,1,0:T(8,128)(2,1)}, u32[]{:S(2)}, u32[]{:S(2)}) collective-permute-start(bf16[8,6,192,192]{3,2,1,0:T(8,128)(2,1)} %constant_dynamic-slice_fusion.1.mid_ref.refs_7_), channel_id=1, source_target_pairs={{0,16},{16,0},{1,17},{17,1},{2,18},{18,2},{3,19},{19,3},{4,20},{20... | collective-permute-start | bytes 10616840 | tf_op jit(solution)/shard_map/ppermute | solution.py:364
  104.8 168.1 %collective-permute-start.5 = (bf16[8,3,192,192]{3,2,1,0:T(8,128)(2,1)}, bf16[8,3,192,192]{3,2,1,0:T(8,128)(2,1)S(1)}, u32[]{:S(2)}, u32[]{:S(2)}) collective-permute-start(bf16[8,3,192,192]{3,2,1,0:T(8,128)(2,1)} %collective-permute-done.2.high_ref.refs_11_), channel_id=1, source_target_pairs={{0,1},{1,2},{2,3},{3,4},{4,5},{5,6},{6,7},{7,8},{8,9},{9,10},{10,1... | collective-permute-start | bytes 5308424 | tf_op jit(solution)/shard_map/ppermute | solution.py:368
  149.9 122.9 %collective-permute-start.6 = (bf16[8,3,192,192]{3,2,1,0:T(8,128)(2,1)}, bf16[8,3,192,192]{3,2,1,0:T(8,128)(2,1)S(1)}, u32[]{:S(2)}, u32[]{:S(2)}) collective-permute-start(bf16[8,3,192,192]{3,2,1,0:T(8,128)(2,1)} %collective-permute-done.low_ref.refs_9_), channel_id=1, source_target_pairs={{0,15},{1,0},{2,1},{3,2},{4,3},{5,4},{6,5},{7,6},{8,7},{9,8},{10,9... | collective-permute-start | bytes 5308424 | tf_op jit(solution)/shard_map/ppermute | solution.py:369
  270.4 182.5 %collective-permute-start.8 = (f32[2,3,192,192]{3,2,1,0:T(8,128)}, f32[2,3,192,192]{3,2,1,0:T(8,128)S(1)}, u32[]{:S(2)}, u32[]{:S(2)}) collective-permute-start(f32[2,3,192,192]{3,2,1,0:T(8,128)} %get-tuple-element.9), channel_id=1, source_target_pairs={{0,15},{1,0},{2,1},{3,2},{4,3},{5,4},{6,5},{7,6},{8,7},{9,8},{10,9... | collective-permute-start | bytes 2654216 | tf_op jit(solution)/shard_map/ppermute | solution.py:377
  272.9 180.0 %collective-permute-start.7 = (f32[2,3,192,192]{3,2,1,0:T(8,128)}, f32[2,3,192,192]{3,2,1,0:T(8,128)}, u32[]{:S(2)}, u32[]{:S(2)}) collective-permute-start(f32[2,3,192,192]{3,2,1,0:T(8,128)} %get-tuple-element.10), channel_id=1, source_target_pairs={{0,1},{1,2},{2,3},{3,4},{4,5},{5,6},{6,7},{7,8},{8,9},{9,10},{10,1... | collective-permute-start | bytes 2654216 | tf_op jit(solution)/shard_map/ppermute | solution.py:376
  272.9 1.4 copy-start.5
  274.3 1.4 copy-start.6
  275.7 121.3 %slice-start = ((s8[4718592]{0:T(1024)(128)(4,1)}), s8[4194304]{0:T(1024)(128)(4,1)S(1)}, s32[]{:S(2)}) async-start(s8[4718592]{0:T(1024)(128)(4,1)} %bitcast.10), calls=%async_computation | async-start | bytes 8388608
  275.7 121.3 %slice-start.1 = ((s8[4718592]{0:T(1024)(128)(4,1)}), s8[524288]{0:T(1024)(128)(4,1)S(1)}, s32[]{:S(2)}) async-start(s8[4718592]{0:T(1024)(128)(4,1)} %bitcast.10), calls=%async_computation.1 | async-start | bytes 1048576
  390.9 6.0 %copy-start.2 = (bf16[8,3,192,192]{3,2,1,0:T(8,128)(2,1)S(1)}, bf16[8,3,192,192]{3,2,1,0:T(8,128)(2,1)}, u32[]{:S(2)}) copy-start(bf16[8,3,192,192]{3,2,1,0:T(8,128)(2,1)} %copy-done.1) | copy-start | bytes 5308420
  394.3 58.6 %collective-permute-start.10 = (f32[2,3,192,192]{3,2,1,0:T(8,128)}, f32[2,3,192,192]{3,2,1,0:T(8,128)}, u32[]{:S(2)}, u32[]{:S(2)}) collective-permute-start(f32[2,3,192,192]{3,2,1,0:T(8,128)} %get-tuple-element.7), channel_id=1, source_target_pairs={{0,15},{1,0},{2,1},{3,2},{4,3},{5,4},{6,5},{7,6},{8,7},{9,8},{10,9... | collective-permute-start | bytes 2654216 | tf_op jit(solution)/shard_map/ppermute | solution.py:377
  397.0 55.9 %collective-permute-start.9 = (f32[2,3,192,192]{3,2,1,0:T(8,128)}, f32[2,3,192,192]{3,2,1,0:T(8,128)}, u32[]{:S(2)}, u32[]{:S(2)}) collective-permute-start(f32[2,3,192,192]{3,2,1,0:T(8,128)} %get-tuple-element.8), channel_id=1, source_target_pairs={{0,1},{1,2},{2,3},{3,4},{4,5},{5,6},{6,7},{7,8},{8,9},{9,10},{10,1... | collective-permute-start | bytes 2654216 | tf_op jit(solution)/shard_map/ppermute | solution.py:376
  405.0 0.7 copy-start.4
  406.7 2.3 copy-start
  417.4 0.7 copy-start.3

commit v2 on v1

--- a/solution.py
+++ b/solution.py
@@ -207,11 +207,8 @@
             lax.fori_loop(0, piece.shape[1], place, 0)
             place_at += piece.shape[1]
 
-    def load(k, carry):
-        start[k + EDGE + 1] = warm_ref[0, 0, 0, k]
-        return carry
-
-    lax.fori_loop(0, planes, load, 0)
+    for k in range(planes):
+        start[k + EDGE + 1] = warm_ref[0, 0, 0, :, k * GY : (k + 1) * GY]
     ring = ring_ref[...]
 
     def swept(field, e, weight):
@@ -243,20 +240,21 @@
     lax.fori_loop(0, (planes + 6) // 2, sweep_three, 0)
 
 
-def window(step, below, pieces, above, targets, warm_start, ring):
+def window(step, orbitals, below, pieces, above, targets, warm_start, ring):
+    first, number = orbitals
     count, planes = targets.shape[:2]
     wide = planes + 2 * EDGE
     parts = (below,) + tuple(pieces) + (above,)
     plane = (GY, GZ)
     grid_spec = pltpu.PrefetchScalarGridSpec(
         num_scalar_prefetch=1,
-        grid=(ORB, count),
+        grid=(number, count),
         in_specs=[
-            pl.BlockSpec((1,) + part.shape[1:], lambda i, j, s: (i, 0, 0, 0)) for part in parts
+            pl.BlockSpec((1,) + part.shape[1:], lambda i, j, s: (first + i, 0, 0, 0)) for part in parts
         ]
         + [
             pl.BlockSpec(targets.shape, lambda i, j, s: (0, 0, 0, 0), pipeline_mode=pl.Buffered(1)),
-            pl.BlockSpec((1, 1, 1, planes) + plane, lambda i, j, s: (s[0], i, j, 0, 0, 0)),
+            pl.BlockSpec((1, 1, 1, GZ, planes * GY), lambda i, j, s: (s[0], first + i, j, 0, 0)),
             pl.BlockSpec(plane, lambda i, j, s: (0, 0), pipeline_mode=pl.Buffered(1)),
         ],
         out_specs=pl.BlockSpec((count, wide) + plane, lambda i, j, s: (0, 0, 0, 0), pipeline_mode=pl.Buffered(1)),
@@ -273,20 +271,20 @@
         grid_spec=grid_spec,
         out_shape=jax.ShapeDtypeStruct((count, wide) + plane, jnp.float32),
         cost_estimate=pl.CostEstimate(
-            flops=ORB * count * 48 * 4 * GY * GY * GZ, bytes_accessed=30_000_000, transcendentals=0
+            flops=number * count * 80 * 4 * GY * GY * GZ, bytes_accessed=4_000_000 * number, transcendentals=0
         ),
         compiler_params=pltpu.CompilerParams(vmem_limit_bytes=56 << 20),
     )(step.reshape(1), *parts, targets, warm_start, ring)
 
 
 def final_kernel(planes, means_ref, *refs):
-    own, remote, own_low, own_high, remote_low, remote_high = refs[:6]
-    pieces = (refs[6:9], refs[9:12])
-    out_ref = refs[12]
+    own, more, remote, own_low, own_high, remote_low, remote_high = refs[:7]
+    pieces = (refs[7:10], refs[10:13])
+    out_ref = refs[13]
     k = pl.program_id(0)
     count = out_ref.shape[0]
     for j in range(count):
-        out_ref[j, 0] = own[j, 0] + remote[j, 0]
+        out_ref[j, 0] = own[j, 0] + more[j, 0] + remote[j, 0]
 
     def constants(which):
         for j in range(count):
@@ -315,7 +313,7 @@
         constants(2)
 
 
-def final_sum(means, own, remote, sides, own_pieces, remote_pieces):
+def final_sum(means, own, more, remote, sides, own_pieces, remote_pieces):
     count, wide = own.shape[:2]
     planes = wide - 2 * EDGE
     plane = (GY, GZ)
@@ -329,23 +327,35 @@
     return pl.pallas_call(
         functools.partial(final_kernel, planes),
         grid=(planes,),
-        in_specs=[pl.BlockSpec(memory_space=pltpu.SMEM), centre, centre] + side + side + piece + piece,
+        in_specs=[pl.BlockSpec(memory_space=pltpu.SMEM), centre, centre, centre] + side + side + piece + piece,
         out_specs=pl.BlockSpec((count, 1) + plane, lambda k: (0, k, 0, 0)),
         out_shape=jax.ShapeDtypeStruct((count, planes) + plane, jnp.float32),
         cost_estimate=pl.CostEstimate(
             flops=40 * count * planes * GY * GZ, bytes_accessed=28_000_000, transcendentals=0
         ),
         compiler_params=pltpu.CompilerParams(vmem_limit_bytes=40 << 20),
-    )(means, own, remote, *sides, *own_pieces, *remote_pieces)
+    )(means, own, more, remote, *sides, *own_pieces, *remote_pieces)
+
+
+def by_plane(field, planes):
+    return field.reshape(field.shape[0], GZ, planes, GY).transpose(0, 2, 1, 3)
+
+
+def shifted_sum(values, shifts, devices):
+    parts = [
+        lax.ppermute(values, "domain", [(d, (d + shift) % devices) for d in range(devices)])
+        for shift in shifts
+    ]
+    return functools.reduce(jnp.add, parts, values)
 
 
 def plane_body(targets, partner_pool, owners, warm_start):
     count, rows = targets.shape[:2]
     planes = rows // GY
     plane = (GY, GZ)
-    targets = targets.reshape((count, planes) + plane)
-    pool = partner_pool.reshape((partner_pool.shape[0], planes) + plane)
-    warm = warm_start.reshape((STEPS, ORB, count, planes) + plane)
+    targets = by_plane(jnp.swapaxes(targets, 1, 2), planes)
+    pool = jnp.swapaxes(partner_pool, 1, 2)
+    warm = jnp.swapaxes(warm_start, 3, 4)
     devices = lax.axis_size("domain")
     upward = [(d, (d + 1) % devices) for d in range(devices)]
     downward = [(d, (d - 1) % devices) for d in range(devices)]
@@ -354,46 +364,55 @@
     own_step = jnp.where(owners[0] == band, 0, 1).astype(jnp.int32)
     mid = planes - 2 * EDGE
 
-    def cut(at, size):
-        return lax.dynamic_slice(pool, (own_step * ORB, at, 0, 0), (ORB, size) + plane)
-
-    own_pieces = (cut(0, EDGE), cut(EDGE, mid), cut(planes - EDGE, EDGE))
+    block = lax.dynamic_slice(pool, (own_step * ORB, 0, 0), (ORB, GZ, rows))
+    block = by_plane(lax.optimization_barrier(block), planes)
+    own_pieces = (block[:, :EDGE], block[:, EDGE : EDGE + mid], block[:, planes - EDGE :])
     low, middle, high = own_pieces
     far_low = lax.ppermute(low, "band", swap)
     far_high = lax.ppermute(high, "band", swap)
     far_mid = lax.ppermute(middle, "band", swap)
-    far_pieces = (far_low, far_mid, far_high)
     below = lax.ppermute(high, "domain", upward)
     above = lax.ppermute(low, "domain", downward)
-    far_below = lax.ppermute(far_high, "domain", upward)
-    far_above = lax.ppermute(far_low, "domain", downward)
 
     index = jnp.arange(GY, dtype=jnp.int32)
     apart = (index[:, None] - index[None, :]) % GY
     ring = ((apart == 1) | (apart == GY - 1)).astype(jnp.bfloat16)
 
     def sent(field):
-        to_above = lax.ppermute(field[:, planes + EDGE :], "domain", upward)
+        to_above = lax.ppermute(field[:, EDGE:], "domain", upward)
         to_below = lax.ppermute(field[:, :EDGE], "domain", downward)
         return (to_above, to_below)
 
+    half = ORB // 2
     own_sums = pair_sums(own_pieces, targets)
-    own = window(own_step, below, own_pieces, above, targets, warm, ring)
-    own_sides = sent(own)
+    below, own_sums = lax.optimization_barrier((below, own_sums))
+    own = window(own_step, (0, half), below, own_pieces, above, targets, warm, ring)
+    far_low, far_high, own = lax.optimization_barrier((far_low, far_high, own))
+    far_below = lax.ppermute(far_high, "domain", upward)
+    far_above = lax.ppermute(far_low, "domain", downward)
+    below, own = lax.optimization_barrier((below, own))
+    more = window(own_step, (half, half), below, own_pieces, above, targets, warm, ring)
+    own_sides = sent(jnp.concatenate([own[:, :EDGE] + more[:, :EDGE], own[:, EDGE + planes :] + more[:, EDGE + planes :]], axis=1))
+    far_mid, more = lax.optimization_barrier((far_mid, more))
+    far_pieces = (far_low, far_mid, far_high)
     far_sums = pair_sums(far_pieces, targets)
-    totals = lax.psum(jnp.concatenate([own_sums, far_sums], axis=0), "domain")
+    totals = jnp.concatenate([own_sums, far_sums], axis=0)
+    totals = shifted_sum(totals, range(1, 4), devices)
+    totals, far_below = lax.optimization_barrier((totals, far_below))
+    totals = shifted_sum(totals, range(4, devices, 4), devices)
     means = totals * (coupling / (2.0 * GX * GY * GZ))
-    far = window(1 - own_step, far_below, far_pieces, far_above, targets, warm, ring)
-    far_sides = sent(far)
-    out = final_sum(means, own, far, own_sides + far_sides, own_pieces, far_pieces)
-    return out.reshape(count, rows, GZ)
+    far = window(1 - own_step, (0, ORB), far_below, far_pieces, far_above, targets, warm, ring)
+    far_sides = sent(jnp.concatenate([far[:, :EDGE], far[:, EDGE + planes :]], axis=1))
+    out = final_sum(means, own, more, far, own_sides + far_sides, own_pieces, far_pieces)
+    out = out.transpose(0, 2, 1, 3).reshape(count, GZ, rows)
+    return jnp.swapaxes(out, 1, 2)
 
 
 def body(targets, partner_pool, owners, warm_start):
     rows = targets.shape[1]
     planes = rows // GY
     whole_planes = rows % GY == 0 and planes % 2 == 0 and planes > 2 * EDGE
-    if whole_planes and GY == GZ and lax.axis_size("band") == 2:
+    if whole_planes and GY == GZ and lax.axis_size("domain") % 4 == 0 and lax.axis_size("band") == 2:
         return plane_body(targets, partner_pool, owners, warm_start)
     return sweep_body(targets, partner_pool, owners, warm_start)
 

time: 485 us -> 452 us (0.932); the launches traced: 477 us -> 450 us
  local copies, waits for them, and re-layouts: 116 us -> 65.6 us
  waiting for transfers between devices: 43.2 us -> 85.2 us
  blocking collectives: 33.8 us -> 0 us
  Pallas kernels: 265 us -> 276 us
    unnamed x21 -> x14, local copies, waits for them, and re-layouts: 94.7 us -> 19.2 us
    ppermute x1, waiting for transfers between devices: 43.2 us -> 0.01 us  [plane_body(): far_low = lax.ppermute(low, 'band', swap)]
    ppermute x2 -> x8, waiting for transfers between devices: 0.01 us -> 36.6 us  [the longest x6 22.5 us: shifted_sum(): lax.ppermute(values, 'domain', [(d, (d + shift) % devices) for d in range...]
    psum x1 -> x0, blocking collectives: 33.8 us -> none  [plane_body(): totals = lax.psum(jnp.concatenate([own_sums, far_sums], axis=0), 'domain')]
    ppermute x1, waiting for transfers between devices: 0.01 us -> 22.8 us  [plane_body(): below = lax.ppermute(high, 'domain', upward)]
    ppermute x1, waiting for transfers between devices: 0.01 us -> 20.2 us  [plane_body(): far_mid = lax.ppermute(middle, 'band', swap)]
    reshape x1 -> x2, local copies, waits for them, and re-layouts: 5.61 us -> 19.4 us  [by_plane(): return field.reshape(field.shape[0], GZ, planes, GY).transpose(0, 2, 1, 3)]
    ppermute x2 -> x8, starting transfers between devices: 0.01 us -> 13 us  [the longest x6 11.2 us: shifted_sum(): lax.ppermute(values, 'domain', [(d, (d + shift) % devices) for d in range...]
  transfers between devices with their start and end apart: 11 -> 17, of which waited for: 1 -> 10; matrix products, arithmetic and copies ran while one was open for 13% -> 4% of each run, Pallas kernels for 52% -> 57%
where the time goes in v2:
time: 452 us; the launch traced here: 450 us
  Pallas kernels  276 us (61%)
  waiting for transfers between devices  85.2 us (19%)
  local copies, waits for them, and re-layouts  65.6 us (15%)
  starting transfers between devices  18.9 us (4%)
    pallas_call x3, Pallas kernels, window(): pl.pallas_call(functools.partial(window_kernel, planes), grid_spec=grid_s...  241 us
    ppermute x1, waiting for transfers between devices, plane_body(): below = lax.ppermute(high, 'domain', upward)  22.8 us
    ppermute x6, waiting for transfers between devices, shifted_sum(): lax.ppermute(values, 'domain', [(d, (d + shift) % devices) for d in range...  22.5 us
    ppermute x1, waiting for transfers between devices, plane_body(): far_mid = lax.ppermute(middle, 'band', swap)  20.2 us
    reshape x2, local copies, waits for them, and re-layouts, by_plane(): return field.reshape(field.shape[0], GZ, planes, GY).transpose(0, 2, 1, 3)  19.4 us
    unnamed x14, local copies, waits for them, and re-layouts  19.2 us
    pallas_call x1, Pallas kernels, final_sum(): pl.pallas_call(functools.partial(final_kernel, planes), grid=(planes,), i...  18.8 us
    pallas_call x2, Pallas kernels, pair_sums(): pl.pallas_call(functools.partial(sums_kernel, planes), grid=(ORB,), in_sp...  16.4 us
  transfers between devices with their start and end apart: 17, of which 10 were waited for; matrix products, arithmetic and copies ran while one was open for 4% of the time, Pallas kernels for 57%

profile of v2, /device:TPU:1, one launch (start us, length us, event | category | flops | bytes accessed | tf_op | source)
XLA Modules:
  0.0 450.3 jit_solution(9312868629790489462)
XLA Ops:
  0.7 6.3 %constant_dynamic-slice_fusion = bf16[8,2304,192]{1,2,0:T(8,128)(2,1)} fusion(bf16[32,2304,192]{1,2,0:T(8,128)(2,1)} %param.5, s32[]{:T(128)S(6)} %select_n.19), kind=kLoop, calls=%fused_computation.14 | loop fusion | bytes 14155780 | tf_op jit(solution)/shard_map/dynamic-slice
  7.0 11.3 %copy.39 = bf16[8,2304,192]{2,1,0:T(8,128)(2,1)} copy(bf16[8,2304,192]{1,2,0:T(8,128)(2,1)} %constant_dynamic-slice_fusion) | data formatting | bytes 14155776
  18.3 13.0 %copy.34 = bf16[8,192,12,192]{3,1,2,0:T(8,128)(2,1)} copy(bf16[8,192,12,192]{1,3,2,0:T(8,128)(2,1)} %bitcast.25) | data formatting | bytes 14155776 | tf_op jit(solution)/shard_map/reshape | solution.py:341
  31.3 4.4 fusion.7
  35.7 2.6 collective-permute-start
  43.5 5.5 %copy.35 = f32[2,2304,192]{2,1,0:T(8,128)} copy(f32[2,2304,192]{1,2,0:T(8,128)} %param.4) | data formatting | bytes 7077888 | tf_op args[0]
  49.0 6.3 %copy.36 = f32[2,192,12,192]{3,1,2,0:T(8,128)} copy(f32[2,192,12,192]{1,3,2,0:T(8,128)} %bitcast.28) | data formatting | bytes 7077888 | tf_op jit(solution)/shard_map/reshape | solution.py:341
  57.7 8.0 %shard_map.46 = f32[8,2,8,192]{3,2,1,0:T(8,128)S(1)} custom-call(bf16[8,3,192,192]{3,2,1,0:T(8,128)(2,1)} %get-tuple-element.30.low_ref.refs_7_, bf16[8,6,192,192]{3,2,1,0:T(8,128)(2,1)} %slice.42.mid_ref.refs_8_, bf16[8,3,192,192]{3,2,1,0:T(8,128)(2,1)S(1)} %get-tuple-element.29.high_ref.refs_9_, f32[2,12,192,192]{3,2,1,0:T(8,128)S(1)} %bitcast.19), custom_call_target="tpu_custom_call" | custom-call | flops 14155776 | bytes 11000000 | tf_op jit(solution)/shard_map/pallas_call | solution.py:131
  66.6 22.8 %collective-permute-done.below_ref = bf16[8,3,192,192]{3,2,1,0:T(8,128)(2,1)} collective-permute-done((bf16[8,3,192,192]{3,2,1,0:T(8,128)(2,1)S(1)}, bf16[8,3,192,192]{3,2,1,0:T(8,128)(2,1)}, u32[]{:S(2)}, u32[]{:S(2)}) %collective-permute-start) | collective-permute-done | bytes 1769504 | tf_op jit(solution)/shard_map/ppermute | solution.py:374
  89.4 3.1 collective-permute-done.3.above_ref
  92.4 62.1 %shard_map.47.refs_0_ = f32[2,18,192,192]{3,2,1,0:T(8,128)} custom-call(s32[1]{0:T(128)} %bitcast.7.step_ref, bf16[8,3,192,192]{3,2,1,0:T(8,128)(2,1)} %collective-permute-done.below_ref, bf16[8,3,192,192]{3,2,1,0:T(8,128)(2,1)} %get-tuple-element.30.low_ref.refs_7_, bf16[8,6,192,192]{3,2,1,0:T(8,128)(2,1)} %slice.42.mid_ref.refs_8_, ...), custom_call_target="tpu_custom_call" | custom-call | flops 18119393280 | bytes 16000000 | tf_op jit(solution)/shard_map/pallas_call | solution.py:269
  155.2 62.1 %shard_map.48.refs_1_ = f32[2,18,192,192]{3,2,1,0:T(8,128)} custom-call(s32[1]{0:T(128)} %bitcast.7.step_ref, bf16[8,3,192,192]{3,2,1,0:T(8,128)(2,1)} %collective-permute-done.below_ref, bf16[8,3,192,192]{3,2,1,0:T(8,128)(2,1)} %get-tuple-element.30.low_ref.refs_7_, bf16[8,6,192,192]{3,2,1,0:T(8,128)(2,1)} %slice.42.mid_ref.refs_8_, ...), custom_call_target="tpu_custom_call" | custom-call | flops 18119393280 | bytes 16000000 | tf_op jit(solution)/shard_map/pallas_call | solution.py:269
  217.2 2.7 slice_add_fusion
  220.0 20.2 %collective-permute-done.4.mid_ref.refs_11_ = bf16[8,6,192,192]{3,2,1,0:T(8,128)(2,1)} collective-permute-done((bf16[8,6,192,192]{3,2,1,0:T(8,128)(2,1)}, bf16[8,6,192,192]{3,2,1,0:T(8,128)(2,1)}, u32[]{:S(2)}, u32[]{:S(2)}) %collective-permute-start.4) | collective-permute-done | bytes 3538976 | tf_op jit(solution)/shard_map/ppermute | solution.py:373
  240.2 8.4 %shard_map.49 = f32[8,2,8,192]{3,2,1,0:T(8,128)S(1)} custom-call(bf16[8,3,192,192]{3,2,1,0:T(8,128)(2,1)} %collective-permute-done.1.low_ref.refs_10_, bf16[8,6,192,192]{3,2,1,0:T(8,128)(2,1)} %collective-permute-done.4.mid_ref.refs_11_, bf16[8,3,192,192]{3,2,1,0:T(8,128)(2,1)} %collective-permute-done.2.high_ref.refs_12_, f32[2,12,192,192]{3,2,1,0:T(8,128)S(1)} %bitcast.22), custom_call_target="tpu_custom_call" | custom-call | flops 14155776 | bytes 11000000 | tf_op jit(solution)/shard_map/pallas_call | solution.py:131
  248.7 5.0 %collective-permute-start.7 = (f32[16,2]{1,0:T(8,128)S(1)}, f32[16,2]{1,0:T(8,128)S(1)}, u32[]{:S(2)}, u32[]{:S(2)}) collective-permute-start(f32[16,2]{1,0:T(8,128)S(1)} %pad_maximum_fusion), channel_id=1, source_target_pairs={{0,3},{1,4},{2,5},{3,6},{4,7},{5,8},{6,9},{7,10},{8,11},{9,12},{10... | collective-permute-start | bytes 392 | tf_op jit(solution)/shard_map/ppermute | solution.py:346
  258.5 12.2 %collective-permute-done.6 = f32[16,2]{1,0:T(8,128)S(1)} collective-permute-done((f32[16,2]{1,0:T(8,128)S(1)}, f32[16,2]{1,0:T(8,128)S(1)}, u32[]{:S(2)}, u32[]{:S(2)}) %collective-permute-start.6) | collective-permute-done | bytes 160 | tf_op jit(solution)/shard_map/ppermute | solution.py:346
  270.8 116.7 %shard_map.50.refs_2_ = f32[2,18,192,192]{3,2,1,0:T(8,128)} custom-call(s32[1]{0:T(128)} %bitcast.9.step_ref, bf16[8,3,192,192]{3,2,1,0:T(8,128)(2,1)} %collective-permute-done.8.below_ref, bf16[8,3,192,192]{3,2,1,0:T(8,128)(2,1)} %collective-permute-done.1.low_ref.refs_10_, bf16[8,6,192,192]{3,2,1,0:T(8,128)(2,1)} %collective-permute-done.4.mid_ref.refs_11_, ...), custom_call_target="tpu_custom_call" | custom-call | flops 36238786560 | bytes 32000000 | tf_op jit(solution)/shard_map/pallas_call | solution.py:269
  394.6 3.1 collective-permute-done.10
  398.7 4.2 collective-permute-done.9
  403.0 14.1 %collective-permute-done.15.refs_5_ = f32[2,3,192,192]{3,2,1,0:T(8,128)S(1)} collective-permute-done((f32[2,3,192,192]{3,2,1,0:T(8,128)S(1)}, f32[2,3,192,192]{3,2,1,0:T(8,128)S(1)}, u32[]{:S(2)}, u32[]{:S(2)}) %collective-permute-start.15) | collective-permute-done | bytes 884768 | tf_op jit(solution)/shard_map/ppermute | solution.py:382
  419.5 18.8 %shard_map.51 = f32[2,12,192,192]{3,2,1,0:T(8,128)} custom-call(f32[16,2]{1,0:T(8,128)S(1)} %add_multiply_fusion.means_ref, f32[2,18,192,192]{3,2,1,0:T(8,128)} %shard_map.47.refs_0_, f32[2,18,192,192]{3,2,1,0:T(8,128)} %shard_map.48.refs_1_, f32[2,18,192,192]{3,2,1,0:T(8,128)} %shard_map.50.refs_2_, f32[2,3,192,192]{3,2,1,0:T(8,128)S(1)} %collective-permute-done.13.refs_3_, ...), custom_call_target="tpu_custom_call" | custom-call | flops 35389440 | bytes 28000000 | tf_op jit(solution)/shard_map/pallas_call | solution.py:327
  438.4 6.3 %copy.37 = f32[2,192,12,192]{1,3,2,0:T(8,128)} copy(f32[2,192,12,192]{3,1,2,0:T(8,128)} %bitcast.26) | data formatting | bytes 7077888 | tf_op jit(solution)/shard_map/transpose | solution.py:407
  444.7 5.6 %copy.38 = f32[2,2304,192]{1,2,0:T(8,128)} copy(f32[2,2304,192]{2,1,0:T(8,128)} %bitcast.27) | data formatting | bytes 7077888 | tf_op jit(solution)/shard_map/transpose | solution.py:408
  (46 shorter events, 24.5 us)
Async XLA Ops:
  31.3 8.4 %copy-start.3 = (bf16[8,192,12,192]{3,1,2,0:T(8,128)(2,1)S(1)}, bf16[8,192,12,192]{3,1,2,0:T(8,128)(2,1)}, u32[]{:S(2)}) copy-start(bf16[8,192,12,192]{3,1,2,0:T(8,128)(2,1)} %copy.34) | copy-start | bytes 21233668
  35.7 19.7 %copy-start.1 = (bf16[8,3,192,192]{3,2,1,0:T(8,128)(2,1)}, bf16[8,3,192,192]{3,2,1,0:T(8,128)(2,1)S(1)}, u32[]{:S(2)}) copy-start(bf16[8,3,192,192]{3,2,1,0:T(8,128)(2,1)S(1)} %get-tuple-element.29.high_ref.refs_9_) | copy-start | bytes 5308420
  35.7 53.7 %collective-permute-start = (bf16[8,3,192,192]{3,2,1,0:T(8,128)(2,1)S(1)}, bf16[8,3,192,192]{3,2,1,0:T(8,128)(2,1)}, u32[]{:S(2)}, u32[]{:S(2)}) collective-permute-start(bf16[8,3,192,192]{3,2,1,0:T(8,128)(2,1)S(1)} %get-tuple-element.29.high_ref.refs_9_), channel_id=1, source_target_pairs={{0,1},{1,2},{2,3},{3,4},{4,5},{5,6},{6,7},{7,8},{8,9},{9,10},{10,1... | collective-permute-start | bytes 5308424 | tf_op jit(solution)/shard_map/ppermute | solution.py:374
  38.3 54.2 %collective-permute-start.3 = (bf16[8,3,192,192]{3,2,1,0:T(8,128)(2,1)}, bf16[8,3,192,192]{3,2,1,0:T(8,128)(2,1)}, u32[]{:S(2)}, u32[]{:S(2)}) collective-permute-start(bf16[8,3,192,192]{3,2,1,0:T(8,128)(2,1)} %get-tuple-element.30.low_ref.refs_7_), channel_id=1, source_target_pairs={{0,15},{1,0},{2,1},{3,2},{4,3},{5,4},{6,5},{7,6},{8,7},{9,8},{10,9... | collective-permute-start | bytes 5308424 | tf_op jit(solution)/shard_map/ppermute | solution.py:375
  38.3 116.3 %collective-permute-start.1 = (bf16[8,3,192,192]{3,2,1,0:T(8,128)(2,1)}, bf16[8,3,192,192]{3,2,1,0:T(8,128)(2,1)}, u32[]{:S(2)}, u32[]{:S(2)}) collective-permute-start(bf16[8,3,192,192]{3,2,1,0:T(8,128)(2,1)} %get-tuple-element.30.low_ref.refs_7_), channel_id=1, source_target_pairs={{0,16},{16,0},{1,17},{17,1},{2,18},{18,2},{3,19},{19,3},{4,20},{20... | collective-permute-start | bytes 5308424 | tf_op jit(solution)/shard_map/ppermute | solution.py:371
  39.5 115.1 %collective-permute-start.2 = (bf16[8,3,192,192]{3,2,1,0:T(8,128)(2,1)S(1)}, bf16[8,3,192,192]{3,2,1,0:T(8,128)(2,1)}, u32[]{:S(2)}, u32[]{:S(2)}) collective-permute-start(bf16[8,3,192,192]{3,2,1,0:T(8,128)(2,1)S(1)} %get-tuple-element.29.high_ref.refs_9_), channel_id=1, source_target_pairs={{0,16},{16,0},{1,17},{17,1},{2,18},{18,2},{3,19},{19,3},{4,20},{20... | collective-permute-start | bytes 5308424 | tf_op jit(solution)/shard_map/ppermute | solution.py:372
  42.2 197.9 %collective-permute-start.4 = (bf16[8,6,192,192]{3,2,1,0:T(8,128)(2,1)}, bf16[8,6,192,192]{3,2,1,0:T(8,128)(2,1)}, u32[]{:S(2)}, u32[]{:S(2)}) collective-permute-start(bf16[8,6,192,192]{3,2,1,0:T(8,128)(2,1)} %slice.42.mid_ref.refs_8_), channel_id=1, source_target_pairs={{0,16},{16,0},{1,17},{17,1},{2,18},{18,2},{3,19},{19,3},{4,20},{20... | collective-permute-start | bytes 10616840 | tf_op jit(solution)/shard_map/ppermute | solution.py:373
  55.3 2.3 copy-start
  92.4 147.7 %slice-start = ((s8[4718592]{0:T(1024)(128)(4,1)}), s8[4194304]{0:T(1024)(128)(4,1)S(1)}, s32[]{:S(2)}) async-start(s8[4718592]{0:T(1024)(128)(4,1)} %bitcast.20), calls=%async_computation | async-start | bytes 8388608
  154.6 85.6 %slice-start.1 = ((s8[4718592]{0:T(1024)(128)(4,1)}), s8[524288]{0:T(1024)(128)(4,1)S(1)}, s32[]{:S(2)}) async-start(s8[4718592]{0:T(1024)(128)(4,1)} %bitcast.20), calls=%async_computation.1 | async-start | bytes 1048576
  154.6 116.2 %collective-permute-start.8 = (bf16[8,3,192,192]{3,2,1,0:T(8,128)(2,1)}, bf16[8,3,192,192]{3,2,1,0:T(8,128)(2,1)}, u32[]{:S(2)}, u32[]{:S(2)}) collective-permute-start(bf16[8,3,192,192]{3,2,1,0:T(8,128)(2,1)} %collective-permute-done.2.high_ref.refs_12_), channel_id=1, source_target_pairs={{0,1},{1,2},{2,3},{3,4},{4,5},{5,6},{6,7},{7,8},{8,9},{9,10},{10,1... | collective-permute-start | bytes 5308424 | tf_op jit(solution)/shard_map/ppermute | solution.py:391
  154.7 116.1 %collective-permute-start.12 = (bf16[8,3,192,192]{3,2,1,0:T(8,128)(2,1)}, bf16[8,3,192,192]{3,2,1,0:T(8,128)(2,1)}, u32[]{:S(2)}, u32[]{:S(2)}) collective-permute-start(bf16[8,3,192,192]{3,2,1,0:T(8,128)(2,1)} %collective-permute-done.1.low_ref.refs_10_), channel_id=1, source_target_pairs={{0,15},{1,0},{2,1},{3,2},{4,3},{5,4},{6,5},{7,6},{8,7},{9,8},{10,9... | collective-permute-start | bytes 5308424 | tf_op jit(solution)/shard_map/ppermute | solution.py:392
  248.7 8.2 %collective-permute-start.7 = (f32[16,2]{1,0:T(8,128)S(1)}, f32[16,2]{1,0:T(8,128)S(1)}, u32[]{:S(2)}, u32[]{:S(2)}) collective-permute-start(f32[16,2]{1,0:T(8,128)S(1)} %pad_maximum_fusion), channel_id=1, source_target_pairs={{0,3},{1,4},{2,5},{3,6},{4,7},{5,8},{6,9},{7,10},{8,11},{9,12},{10... | collective-permute-start | bytes 392 | tf_op jit(solution)/shard_map/ppermute | solution.py:346
  253.7 149.2 %collective-permute-start.13 = (f32[2,3,192,192]{3,2,1,0:T(8,128)S(1)}, f32[2,3,192,192]{3,2,1,0:T(8,128)S(1)}, u32[]{:S(2)}, u32[]{:S(2)}) collective-permute-start(f32[2,3,192,192]{3,2,1,0:T(8,128)S(1)} %get-tuple-element.28), channel_id=1, source_target_pairs={{0,1},{1,2},{2,3},{3,4},{4,5},{5,6},{6,7},{7,8},{8,9},{9,10},{10,1... | collective-permute-start | bytes 2654216 | tf_op jit(solution)/shard_map/ppermute | solution.py:382
  253.7 17.0 %collective-permute-start.6 = (f32[16,2]{1,0:T(8,128)S(1)}, f32[16,2]{1,0:T(8,128)S(1)}, u32[]{:S(2)}, u32[]{:S(2)}) collective-permute-start(f32[16,2]{1,0:T(8,128)S(1)} %pad_maximum_fusion), channel_id=1, source_target_pairs={{0,2},{1,3},{2,4},{3,5},{4,6},{5,7},{6,8},{7,9},{8,10},{9,11},{10,... | collective-permute-start | bytes 392 | tf_op jit(solution)/shard_map/ppermute | solution.py:346
  256.9 13.9 %collective-permute-start.5 = (f32[16,2]{1,0:T(8,128)S(1)}, f32[16,2]{1,0:T(8,128)S(1)}, u32[]{:S(2)}, u32[]{:S(2)}) collective-permute-start(f32[16,2]{1,0:T(8,128)S(1)} %pad_maximum_fusion), channel_id=1, source_target_pairs={{0,1},{1,2},{2,3},{3,4},{4,5},{5,6},{6,7},{7,8},{8,9},{9,10},{10,1... | collective-permute-start | bytes 392 | tf_op jit(solution)/shard_map/ppermute | solution.py:346
  270.7 132.2 %collective-permute-start.14 = (f32[2,3,192,192]{3,2,1,0:T(8,128)S(1)}, f32[2,3,192,192]{3,2,1,0:T(8,128)S(1)}, u32[]{:S(2)}, u32[]{:S(2)}) collective-permute-start(f32[2,3,192,192]{3,2,1,0:T(8,128)S(1)} %get-tuple-element.27), channel_id=1, source_target_pairs={{0,15},{1,0},{2,1},{3,2},{4,3},{5,4},{6,5},{7,6},{8,7},{9,8},{10,9... | collective-permute-start | bytes 2654216 | tf_op jit(solution)/shard_map/ppermute | solution.py:383
  387.5 32.0 %copy-start.2 = (bf16[8,3,192,192]{3,2,1,0:T(8,128)(2,1)S(1)}, bf16[8,3,192,192]{3,2,1,0:T(8,128)(2,1)}, u32[]{:S(2)}) copy-start(bf16[8,3,192,192]{3,2,1,0:T(8,128)(2,1)} %copy-done.1) | copy-start | bytes 5308420
  389.5 27.6 %collective-permute-start.15 = (f32[2,3,192,192]{3,2,1,0:T(8,128)S(1)}, f32[2,3,192,192]{3,2,1,0:T(8,128)S(1)}, u32[]{:S(2)}, u32[]{:S(2)}) collective-permute-start(f32[2,3,192,192]{3,2,1,0:T(8,128)S(1)} %get-tuple-element.32), channel_id=1, source_target_pairs={{0,1},{1,2},{2,3},{3,4},{4,5},{5,6},{6,7},{7,8},{8,9},{9,10},{10,1... | collective-permute-start | bytes 2654216 | tf_op jit(solution)/shard_map/ppermute | solution.py:382
  391.3 28.3 %collective-permute-start.16 = (f32[2,3,192,192]{3,2,1,0:T(8,128)S(1)}, f32[2,3,192,192]{3,2,1,0:T(8,128)S(1)}, u32[]{:S(2)}, u32[]{:S(2)}) collective-permute-start(f32[2,3,192,192]{3,2,1,0:T(8,128)S(1)} %get-tuple-element.31), channel_id=1, source_target_pairs={{0,15},{1,0},{2,1},{3,2},{4,3},{5,4},{6,5},{7,6},{8,7},{9,8},{10,9... | collective-permute-start | bytes 2654216 | tf_op jit(solution)/shard_map/ppermute | solution.py:383
  391.3 2.6 collective-permute-start.11
  393.9 3.8 collective-permute-start.10
  397.7 5.2 %collective-permute-start.9 = (f32[16,2]{1,0:T(8,128)S(1)}, f32[16,2]{1,0:T(8,128)S(1)}, u32[]{:S(2)}, u32[]{:S(2)}) collective-permute-start(f32[16,2]{1,0:T(8,128)S(1)} %add_add_fusion), channel_id=1, source_target_pairs={{0,4},{1,5},{2,6},{3,7},{4,8},{5,9},{6,10},{7,11},{8,12},{9,13},{1... | collective-permute-start | bytes 392 | tf_op jit(solution)/shard_map/ppermute | solution.py:346

commit v3 on v2

--- a/solution.py
+++ b/solution.py
@@ -365,12 +365,16 @@
     mid = planes - 2 * EDGE
 
     block = lax.dynamic_slice(pool, (own_step * ORB, 0, 0), (ORB, GZ, rows))
-    block = by_plane(lax.optimization_barrier(block), planes)
+    block = lax.optimization_barrier(block)
+    sides = EDGE * GY
+    swapped = [
+        by_plane(lax.ppermute(part, "band", swap), part.shape[2] // GY)
+        for part in (block[:, :, :sides], block[:, :, rows - sides :], block[:, :, sides : rows - sides])
+    ]
+    far_low, far_high, far_mid = swapped
+    block = by_plane(block, planes)
     own_pieces = (block[:, :EDGE], block[:, EDGE : EDGE + mid], block[:, planes - EDGE :])
-    low, middle, high = own_pieces
-    far_low = lax.ppermute(low, "band", swap)
-    far_high = lax.ppermute(high, "band", swap)
-    far_mid = lax.ppermute(middle, "band", swap)
+    low, _, high = own_pieces
     below = lax.ppermute(high, "domain", upward)
     above = lax.ppermute(low, "domain", downward)
 
@@ -398,8 +402,8 @@
     far_sums = pair_sums(far_pieces, targets)
     totals = jnp.concatenate([own_sums, far_sums], axis=0)
     totals = shifted_sum(totals, range(1, 4), devices)
+    totals = shifted_sum(totals, range(4, devices, 4), devices)
     totals, far_below = lax.optimization_barrier((totals, far_below))
-    totals = shifted_sum(totals, range(4, devices, 4), devices)
     means = totals * (coupling / (2.0 * GX * GY * GZ))
     far = window(1 - own_step, (0, ORB), far_below, far_pieces, far_above, targets, warm, ring)
     far_sides = sent(jnp.concatenate([far[:, :EDGE], far[:, EDGE + planes :]], axis=1))

time: 452 us -> 487 us (1.077)
  local copies, waits for them, and re-layouts: 65.6 us -> 125 us
  waiting for transfers between devices: 85.2 us -> 48.5 us
  starting transfers between devices: 18.9 us -> 31.2 us
    ppermute x1, waiting for transfers between devices: 22.8 us -> 0.01 us  [plane_body(): below = lax.ppermute(high, 'domain', upward)]
    slice x1 -> x6, local copies, waits for them, and re-layouts: 4.35 us -> 27 us  [the longest x2 11.2 us: plane_body(): block[:, :, sides:rows - sides]]
    ppermute x6, waiting for transfers between devices: 22.5 us -> 6.96 us  [shifted_sum(): lax.ppermute(values, 'domain', [(d, (d + shift) % devices) for d in range...]
    ppermute x0 -> x3, local copies, waits for them, and re-layouts: none -> 14.7 us  [plane_body(): lax.ppermute(part, 'band', swap)]
    reshape x2 -> x5, local copies, waits for them, and re-layouts: 19.4 us -> 33.6 us  [by_plane(): return field.reshape(field.shape[0], GZ, planes, GY).transpose(0, 2, 1, 3)]
    ppermute x2, starting transfers between devices: 0.01 us -> 10.7 us  [sent(): to_below = lax.ppermute(field[:, :EDGE], 'domain', downward)]
    ppermute x2, waiting for transfers between devices: 2.48 us -> 11.8 us  [sent(): to_below = lax.ppermute(field[:, :EDGE], 'domain', downward)]
    ppermute x3, waiting for transfers between devices: 20.2 us -> 14.3 us  [plane_body(): lax.ppermute(part, 'band', swap)]
  transfers between devices with their start and end apart: 17 -> 17, of which waited for: 10 -> 7; matrix products, arithmetic and copies ran while one was open for 4% -> 17% of each run, Pallas kernels for 57% -> 53%
where the time goes in v3:
time: 487 us; the launch traced here: 485 us
  Pallas kernels  274 us (56%)
  local copies, waits for them, and re-layouts  125 us (26%)
  waiting for transfers between devices  48.5 us (10%)
  starting transfers between devices  31.2 us (6%)
  other arithmetic  5.06 us (1%)
    pallas_call x3, Pallas kernels, window(): pl.pallas_call(functools.partial(window_kernel, planes), grid_spec=grid_s...  241 us
    reshape x5, local copies, waits for them, and re-layouts, by_plane(): return field.reshape(field.shape[0], GZ, planes, GY).transpose(0, 2, 1, 3)  33.6 us
    unnamed x16, local copies, waits for them, and re-layouts  24.1 us
    pallas_call x1, Pallas kernels, final_sum(): pl.pallas_call(functools.partial(final_kernel, planes), grid=(planes,), i...  18.9 us
    ppermute x2, waiting for transfers between devices, sent(): to_above = lax.ppermute(field[:, EDGE:], 'domain', upward)  15.5 us
    ppermute x3, local copies, waits for them, and re-layouts, plane_body(): lax.ppermute(part, 'band', swap)  14.7 us
    pallas_call x2, Pallas kernels, pair_sums(): pl.pallas_call(functools.partial(sums_kernel, planes), grid=(ORB,), in_sp...  14.7 us
    ppermute x3, waiting for transfers between devices, plane_body(): lax.ppermute(part, 'band', swap)  14.3 us
  transfers between devices with their start and end apart: 17, of which 7 were waited for; matrix products, arithmetic and copies ran while one was open for 17% of the time, Pallas kernels for 53%

profile of v3, /device:TPU:1, one launch (start us, length us, event | category | flops | bytes accessed | tf_op | source)
XLA Modules:
  0.0 484.8 jit_solution(8736447852607729137)
XLA Ops:
  0.7 6.3 %constant_dynamic-slice_fusion = bf16[8,2304,192]{1,2,0:T(8,128)(2,1)} fusion(bf16[32,2304,192]{1,2,0:T(8,128)(2,1)} %param.5, s32[]{:T(128)S(6)} %select_n.19), kind=kLoop, calls=%fused_computation.15 | loop fusion | bytes 14155780 | tf_op jit(solution)/shard_map/dynamic-slice
  7.0 11.3 %copy.69 = bf16[8,2304,192]{2,1,0:T(8,128)(2,1)} copy(bf16[8,2304,192]{1,2,0:T(8,128)(2,1)} %constant_dynamic-slice_fusion) | data formatting | bytes 14155776
  22.4 4.2 copy.58
  31.1 13.0 %copy.55 = bf16[8,192,12,192]{3,1,2,0:T(8,128)(2,1)} copy(bf16[8,192,12,192]{1,3,2,0:T(8,128)(2,1)} %bitcast.35) | data formatting | bytes 14155776 | tf_op jit(solution)/shard_map/reshape | solution.py:341
  44.2 5.0 %fusion.7 = (bf16[8,3,192,192]{3,2,1,0:T(8,128)(2,1)}, bf16[8,3,192,192]{3,2,1,0:T(8,128)(2,1)}) fusion(bf16[8,12,192,192]{3,2,1,0:T(8,128)(2,1)} %bitcast.37), kind=kLoop, calls=%fused_computation.16 | loop fusion | bytes 7077888 | tf_op jit(solution)/shard_map/slice | solution.py:376
  51.7 4.8 %slice.57 = bf16[8,192,1152]{1,2,0:T(8,128)(2,1)} slice(bf16[8,192,2304]{1,2,0:T(8,128)(2,1)} %bitcast.36), slice={[0:8], [0:192], [576:1728]} | slice | bytes 7077888 | tf_op jit(solution)/shard_map/slice | solution.py:372
  56.6 6.4 %copy.64 = bf16[8,192,1152]{2,1,0:T(8,128)(2,1)} copy(bf16[8,192,1152]{1,2,0:T(8,128)(2,1)} %slice.57) | data formatting | bytes 7077888 | tf_op jit(solution)/shard_map/slice | solution.py:372
  64.2 5.2 %slice.54.mid_ref.refs_8_ = bf16[8,6,192,192]{3,2,1,0:T(8,128)(2,1)} slice(bf16[8,12,192,192]{3,2,1,0:T(8,128)(2,1)} %bitcast.38), slice={[0:8], [3:9], [0:192], [0:192]} | slice | bytes 7077888 | tf_op jit(solution)/shard_map/slice | solution.py:376
  72.8 6.3 %copy.57 = f32[2,192,12,192]{3,1,2,0:T(8,128)} copy(f32[2,192,12,192]{1,3,2,0:T(8,128)} %bitcast.42) | data formatting | bytes 7077888 | tf_op jit(solution)/shard_map/reshape | solution.py:341
  83.8 7.5 %shard_map.46 = f32[8,2,8,192]{3,2,1,0:T(8,128)S(1)} custom-call(bf16[8,3,192,192]{3,2,1,0:T(8,128)(2,1)} %get-tuple-element.29.low_ref.refs_7_, bf16[8,6,192,192]{3,2,1,0:T(8,128)(2,1)S(1)} %copy-done, bf16[8,3,192,192]{3,2,1,0:T(8,128)(2,1)} %get-tuple-element.30.high_ref.refs_9_, f32[2,12,192,192]{3,2,1,0:T(8,128)S(1)} %bitcast.28), custom_call_target="tpu_custom_call" | custom-call | flops 14155776 | bytes 11000000 | tf_op jit(solution)/shard_map/pallas_call | solution.py:131
  99.4 14.3 %collective-permute-done.2 = bf16[8,192,576]{2,1,0:T(8,128)(2,1)} collective-permute-done((bf16[8,192,576]{2,1,0:T(8,128)(2,1)}, bf16[8,192,576]{2,1,0:T(8,128)(2,1)}, u32[]{:S(2)}, u32[]{:S(2)}) %collective-permute-start.2) | collective-permute-done | bytes 1769504 | tf_op jit(solution)/shard_map/ppermute | solution.py:371
  117.9 4.5 copy.63
  122.4 62.0 %shard_map.47.refs_0_ = f32[2,18,192,192]{3,2,1,0:T(8,128)} custom-call(s32[1]{0:T(128)} %bitcast.11.step_ref, bf16[8,3,192,192]{3,2,1,0:T(8,128)(2,1)} %collective-permute-done.below_ref, bf16[8,3,192,192]{3,2,1,0:T(8,128)(2,1)} %get-tuple-element.29.low_ref.refs_7_, bf16[8,6,192,192]{3,2,1,0:T(8,128)(2,1)} %slice.54.mid_ref.refs_8_, ...), custom_call_target="tpu_custom_call" | custom-call | flops 18119393280 | bytes 16000000 | tf_op jit(solution)/shard_map/pallas_call | solution.py:269
  188.1 62.1 %shard_map.48.refs_1_ = f32[2,18,192,192]{3,2,1,0:T(8,128)} custom-call(s32[1]{0:T(128)} %bitcast.11.step_ref, bf16[8,3,192,192]{3,2,1,0:T(8,128)(2,1)} %collective-permute-done.below_ref, bf16[8,3,192,192]{3,2,1,0:T(8,128)(2,1)} %get-tuple-element.29.low_ref.refs_7_, bf16[8,6,192,192]{3,2,1,0:T(8,128)(2,1)} %slice.54.mid_ref.refs_8_, ...), custom_call_target="tpu_custom_call" | custom-call | flops 18119393280 | bytes 16000000 | tf_op jit(solution)/shard_map/pallas_call | solution.py:269
  254.3 6.3 %copy.65 = bf16[8,192,1152]{1,2,0:T(8,128)(2,1)} copy(bf16[8,192,1152]{2,1,0:T(8,128)(2,1)} %collective-permute-done.4) | data formatting | bytes 7077888 | tf_op jit(solution)/shard_map/ppermute | solution.py:371
  260.6 6.8 %copy.66 = bf16[8,192,6,192]{3,1,2,0:T(8,128)(2,1)} copy(bf16[8,192,6,192]{1,3,2,0:T(8,128)(2,1)} %bitcast.40) | data formatting | bytes 7077888 | tf_op jit(solution)/shard_map/reshape | solution.py:341
  272.1 7.1 %shard_map.49 = f32[8,2,8,192]{3,2,1,0:T(8,128)S(1)} custom-call(bf16[8,3,192,192]{3,2,1,0:T(8,128)(2,1)S(1)} %bitcast.31, bf16[8,6,192,192]{3,2,1,0:T(8,128)(2,1)S(1)} %bitcast.24, bf16[8,3,192,192]{3,2,1,0:T(8,128)(2,1)} %bitcast.10.high_ref.refs_12_, f32[2,12,192,192]{3,2,1,0:T(8,128)S(1)} %bitcast.29), custom_call_target="tpu_custom_call" | custom-call | flops 14155776 | bytes 11000000 | tf_op jit(solution)/shard_map/pallas_call | solution.py:131
  294.5 116.8 %shard_map.50.refs_2_ = f32[2,18,192,192]{3,2,1,0:T(8,128)} custom-call(s32[1]{0:T(128)} %bitcast.15.step_ref, bf16[8,3,192,192]{3,2,1,0:T(8,128)(2,1)} %collective-permute-done.11.below_ref, bf16[8,3,192,192]{3,2,1,0:T(8,128)(2,1)} %bitcast.32, bf16[8,6,192,192]{3,2,1,0:T(8,128)(2,1)} %bitcast.22, bf16[8,3,192,192]{3,2,1,0:T(8,128)(2,1)} %bitcast.10.high_ref.refs_12_, ...), custom_call_target="tpu_custom_call" | custom-call | flops 36238786560 | bytes 32000000 | tf_op jit(solution)/shard_map/pallas_call | solution.py:269
  416.4 10.3 %collective-permute-start.16 = (f32[2,3,192,192]{3,2,1,0:T(8,128)S(1)}, f32[2,3,192,192]{3,2,1,0:T(8,128)S(1)}, u32[]{:S(2)}, u32[]{:S(2)}) collective-permute-start(f32[2,3,192,192]{3,2,1,0:T(8,128)S(1)} %get-tuple-element.33), channel_id=1, source_target_pairs={{0,15},{1,0},{2,1},{3,2},{4,3},{5,4},{6,5},{7,6},{8,7},{9,8},{10,9... | collective-permute-start | bytes 2654216 | tf_op jit(solution)/shard_map/ppermute | solution.py:387
  426.7 15.5 %collective-permute-done.15.refs_5_ = f32[2,3,192,192]{3,2,1,0:T(8,128)S(1)} collective-permute-done((f32[2,3,192,192]{3,2,1,0:T(8,128)S(1)}, f32[2,3,192,192]{3,2,1,0:T(8,128)S(1)}, u32[]{:S(2)}, u32[]{:S(2)}) %collective-permute-start.15) | collective-permute-done | bytes 884768 | tf_op jit(solution)/shard_map/ppermute | solution.py:386
  442.2 11.7 %collective-permute-done.16.refs_6_ = f32[2,3,192,192]{3,2,1,0:T(8,128)S(1)} collective-permute-done((f32[2,3,192,192]{3,2,1,0:T(8,128)S(1)}, f32[2,3,192,192]{3,2,1,0:T(8,128)S(1)}, u32[]{:S(2)}, u32[]{:S(2)}) %collective-permute-start.16) | collective-permute-done | bytes 884768 | tf_op jit(solution)/shard_map/ppermute | solution.py:387
  454.0 18.9 %shard_map.51 = f32[2,12,192,192]{3,2,1,0:T(8,128)} custom-call(f32[16,2]{1,0:T(8,128)S(1)} %broadcast_multiply_fusion.means_ref, f32[2,18,192,192]{3,2,1,0:T(8,128)} %shard_map.47.refs_0_, f32[2,18,192,192]{3,2,1,0:T(8,128)} %shard_map.48.refs_1_, f32[2,18,192,192]{3,2,1,0:T(8,128)} %shard_map.50.refs_2_, ...), custom_call_target="tpu_custom_call" | custom-call | flops 35389440 | bytes 28000000 | tf_op jit(solution)/shard_map/pallas_call | solution.py:327
  472.9 6.3 %copy.67 = f32[2,192,12,192]{1,3,2,0:T(8,128)} copy(f32[2,192,12,192]{3,1,2,0:T(8,128)} %bitcast.39) | data formatting | bytes 7077888 | tf_op jit(solution)/shard_map/transpose | solution.py:411
  479.2 5.6 %copy.68 = f32[2,2304,192]{1,2,0:T(8,128)} copy(f32[2,2304,192]{2,1,0:T(8,128)} %bitcast.41) | data formatting | bytes 7077888 | tf_op jit(solution)/shard_map/transpose | solution.py:412
  (59 shorter events, 65.7 us)
Async XLA Ops:
  26.6 65.6 %collective-permute-start.1 = (bf16[8,192,576]{2,1,0:T(8,128)(2,1)}, bf16[8,192,576]{2,1,0:T(8,128)(2,1)}, u32[]{:S(2)}, u32[]{:S(2)}) collective-permute-start(bf16[8,192,576]{2,1,0:T(8,128)(2,1)} %copy.58), channel_id=1, source_target_pairs={{0,16},{16,0},{1,17},{17,1},{2,18},{18,2},{3,19},{19,3},{4,20},{20... | collective-permute-start | bytes 5308424 | tf_op jit(solution)/shard_map/ppermute | solution.py:371
  31.1 82.6 %collective-permute-start.2 = (bf16[8,192,576]{2,1,0:T(8,128)(2,1)}, bf16[8,192,576]{2,1,0:T(8,128)(2,1)}, u32[]{:S(2)}, u32[]{:S(2)}) collective-permute-start(bf16[8,192,576]{2,1,0:T(8,128)(2,1)} %copy.61), channel_id=1, source_target_pairs={{0,16},{16,0},{1,17},{17,1},{2,18},{18,2},{3,19},{19,3},{4,20},{20... | collective-permute-start | bytes 5308424 | tf_op jit(solution)/shard_map/ppermute | solution.py:371
  49.2 73.2 %collective-permute-start = (bf16[8,3,192,192]{3,2,1,0:T(8,128)(2,1)}, bf16[8,3,192,192]{3,2,1,0:T(8,128)(2,1)}, u32[]{:S(2)}, u32[]{:S(2)}) collective-permute-start(bf16[8,3,192,192]{3,2,1,0:T(8,128)(2,1)} %get-tuple-element.30.high_ref.refs_9_), channel_id=1, source_target_pairs={{0,1},{1,2},{2,3},{3,4},{4,5},{5,6},{6,7},{7,8},{8,9},{9,10},{10,1... | collective-permute-start | bytes 5308424 | tf_op jit(solution)/shard_map/ppermute | solution.py:378
  51.7 70.6 %collective-permute-start.3 = (bf16[8,3,192,192]{3,2,1,0:T(8,128)(2,1)}, bf16[8,3,192,192]{3,2,1,0:T(8,128)(2,1)}, u32[]{:S(2)}, u32[]{:S(2)}) collective-permute-start(bf16[8,3,192,192]{3,2,1,0:T(8,128)(2,1)} %get-tuple-element.29.low_ref.refs_7_), channel_id=1, source_target_pairs={{0,15},{1,0},{2,1},{3,2},{4,3},{5,4},{6,5},{7,6},{8,7},{9,8},{10,9... | collective-permute-start | bytes 5308424 | tf_op jit(solution)/shard_map/ppermute | solution.py:379
  63.0 191.3 %collective-permute-start.4 = (bf16[8,192,1152]{2,1,0:T(8,128)(2,1)}, bf16[8,192,1152]{2,1,0:T(8,128)(2,1)}, u32[]{:S(2)}, u32[]{:S(2)}) collective-permute-start(bf16[8,192,1152]{2,1,0:T(8,128)(2,1)} %copy.64), channel_id=1, source_target_pairs={{0,16},{16,0},{1,17},{17,1},{2,18},{18,2},{3,19},{19,3},{4,20},{20... | collective-permute-start | bytes 10616840 | tf_op jit(solution)/shard_map/ppermute | solution.py:371
  64.2 5.2 %copy-start.6 = (f32[2,2304,192]{1,2,0:T(8,128)S(1)}, f32[2,2304,192]{1,2,0:T(8,128)}, u32[]{:S(2)}) copy-start(f32[2,2304,192]{1,2,0:T(8,128)} %param.4) | copy-start | bytes 10616836
  79.1 2.3 copy-start
  81.5 2.3 copy-start.2
  99.4 168.0 %copy-start.4 = (bf16[8,192,3,192]{3,1,2,0:T(8,128)(2,1)}, bf16[8,192,3,192]{3,1,2,0:T(8,128)(2,1)S(1)}, u32[]{:S(2)}) copy-start(bf16[8,192,3,192]{3,1,2,0:T(8,128)(2,1)S(1)} %copy.60) | copy-start | bytes 5308420
  184.4 110.1 %collective-permute-start.11 = (bf16[8,3,192,192]{3,2,1,0:T(8,128)(2,1)}, bf16[8,3,192,192]{3,2,1,0:T(8,128)(2,1)}, u32[]{:S(2)}, u32[]{:S(2)}) collective-permute-start(bf16[8,3,192,192]{3,2,1,0:T(8,128)(2,1)} %bitcast.10.high_ref.refs_12_), channel_id=1, source_target_pairs={{0,1},{1,2},{2,3},{3,4},{4,5},{5,6},{6,7},{7,8},{8,9},{9,10},{10,1... | collective-permute-start | bytes 5308424 | tf_op jit(solution)/shard_map/ppermute | solution.py:395
  188.1 106.4 %collective-permute-start.12 = (bf16[8,3,192,192]{3,2,1,0:T(8,128)(2,1)S(1)}, bf16[8,3,192,192]{3,2,1,0:T(8,128)(2,1)}, u32[]{:S(2)}, u32[]{:S(2)}) collective-permute-start(bf16[8,3,192,192]{3,2,1,0:T(8,128)(2,1)S(1)} %bitcast.30), channel_id=1, source_target_pairs={{0,15},{1,0},{2,1},{3,2},{4,3},{5,4},{6,5},{7,6},{8,7},{9,8},{10,9... | collective-permute-start | bytes 5308424 | tf_op jit(solution)/shard_map/ppermute | solution.py:396
  267.4 2.3 copy-start.1
  269.7 2.3 copy-start.3
  279.3 6.1 %collective-permute-start.7 = (f32[16,2]{1,0:T(8,128)S(1)}, f32[16,2]{1,0:T(8,128)S(1)}, u32[]{:S(2)}, u32[]{:S(2)}) collective-permute-start(f32[16,2]{1,0:T(8,128)S(1)} %pad_maximum_fusion), channel_id=1, source_target_pairs={{0,3},{1,4},{2,5},{3,6},{4,7},{5,8},{6,9},{7,10},{8,11},{9,12},{10... | collective-permute-start | bytes 392 | tf_op jit(solution)/shard_map/ppermute | solution.py:346
  282.1 5.2 %collective-permute-start.6 = (f32[16,2]{1,0:T(8,128)S(1)}, f32[16,2]{1,0:T(8,128)S(1)}, u32[]{:S(2)}, u32[]{:S(2)}) collective-permute-start(f32[16,2]{1,0:T(8,128)S(1)} %pad_maximum_fusion), channel_id=1, source_target_pairs={{0,2},{1,3},{2,4},{3,5},{4,6},{5,7},{6,8},{7,9},{8,10},{9,11},{10,... | collective-permute-start | bytes 392 | tf_op jit(solution)/shard_map/ppermute | solution.py:346
  282.4 4.9 %collective-permute-start.5 = (f32[16,2]{1,0:T(8,128)S(1)}, f32[16,2]{1,0:T(8,128)S(1)}, u32[]{:S(2)}, u32[]{:S(2)}) collective-permute-start(f32[16,2]{1,0:T(8,128)S(1)} %pad_maximum_fusion), channel_id=1, source_target_pairs={{0,1},{1,2},{2,3},{3,4},{4,5},{5,6},{6,7},{7,8},{8,9},{9,10},{10,1... | collective-permute-start | bytes 392 | tf_op jit(solution)/shard_map/ppermute | solution.py:346
  287.3 2.9 collective-permute-start.10
  288.8 138.0 %collective-permute-start.13 = (f32[2,3,192,192]{3,2,1,0:T(8,128)}, f32[2,3,192,192]{3,2,1,0:T(8,128)S(1)}, u32[]{:S(2)}, u32[]{:S(2)}) collective-permute-start(f32[2,3,192,192]{3,2,1,0:T(8,128)} %get-tuple-element.28), channel_id=1, source_target_pairs={{0,1},{1,2},{2,3},{3,4},{4,5},{5,6},{6,7},{7,8},{8,9},{9,10},{10,1... | collective-permute-start | bytes 2654216 | tf_op jit(solution)/shard_map/ppermute | solution.py:386
  290.2 3.8 collective-permute-start.9
  290.2 4.3 collective-permute-start.8
  294.0 132.8 %collective-permute-start.14 = (f32[2,3,192,192]{3,2,1,0:T(8,128)}, f32[2,3,192,192]{3,2,1,0:T(8,128)S(1)}, u32[]{:S(2)}, u32[]{:S(2)}) collective-permute-start(f32[2,3,192,192]{3,2,1,0:T(8,128)} %get-tuple-element.27), channel_id=1, source_target_pairs={{0,15},{1,0},{2,1},{3,2},{4,3},{5,4},{6,5},{7,6},{8,7},{9,8},{10,9... | collective-permute-start | bytes 2654216 | tf_op jit(solution)/shard_map/ppermute | solution.py:387
  411.3 42.7 %copy-start.5 = (bf16[8,192,3,192]{3,1,2,0:T(8,128)(2,1)S(1)}, bf16[8,192,3,192]{3,1,2,0:T(8,128)(2,1)}, u32[]{:S(2)}) copy-start(bf16[8,192,3,192]{3,1,2,0:T(8,128)(2,1)} %copy-done.4) | copy-start | bytes 5308420
  413.4 28.9 %collective-permute-start.15 = (f32[2,3,192,192]{3,2,1,0:T(8,128)S(1)}, f32[2,3,192,192]{3,2,1,0:T(8,128)S(1)}, u32[]{:S(2)}, u32[]{:S(2)}) collective-permute-start(f32[2,3,192,192]{3,2,1,0:T(8,128)S(1)} %get-tuple-element.34), channel_id=1, source_target_pairs={{0,1},{1,2},{2,3},{3,4},{4,5},{5,6},{6,7},{7,8},{8,9},{9,10},{10,1... | collective-permute-start | bytes 2654216 | tf_op jit(solution)/shard_map/ppermute | solution.py:386
  416.4 37.5 %collective-permute-start.16 = (f32[2,3,192,192]{3,2,1,0:T(8,128)S(1)}, f32[2,3,192,192]{3,2,1,0:T(8,128)S(1)}, u32[]{:S(2)}, u32[]{:S(2)}) collective-permute-start(f32[2,3,192,192]{3,2,1,0:T(8,128)S(1)} %get-tuple-element.33), channel_id=1, source_target_pairs={{0,15},{1,0},{2,1},{3,2},{4,3},{5,4},{6,5},{7,6},{8,7},{9,8},{10,9... | collective-permute-start | bytes 2654216 | tf_op jit(solution)/shard_map/ppermute | solution.py:387
